TPU v7x, 32 devices: a whole 2x2x4 slice. The times are simulated.
32 devices in a mesh: gx: 4 (over z), gy: 8 (over y, x, core).
Axes of the slice: x: 2, y: 2, z: 4, core: 2. Of those that a mesh axis runs over, the one named last changes fastest.
Arguments:
- leaf_front: float32 [6144, 12288], P('gx', 'gy'), may hold values from -18 to 18, as said below
- place_pairs: int32 [4, 64], P('gx', 'gy'), may hold values from 0 to 11, as said below
- place_quads: int32 [4, 64], P('gx', 'gy'), may hold values from 0 to 11, as said below
Outputs:
- pair_panel: float32 [6144, 4096], P('gx', 'gy')
- quad_panel: float32 [6144, 4096], P('gx', 'gy')
- quad_update: float32 [4096, 8192], P('gx', 'gy')
Inputs may be any that keep to these rules, and one draw needn't show every extreme that they name: `leaf_front`: each tile is symmetric positive definite. `place_pairs`: each device's 8 entries are distinct; the two devices (q, j) and (q + 2, j) both name blocks 0 to 3, and each names 4 of the other blocks that the other does not name. `place_quads`: devices (q, j) and (q + 2, j) hold equal rows; each row's 8 entries are distinct; the rows of (q, r) and (q, r + 4) both name blocks 0 to 3, and each names 4 of the other blocks that the other does not name.
All inputs are finite; a program needn't handle non-finite values.
Results may differ from a plain program's by a relative error of at most 0.0003.
Values sent between devices are 32-bit elements; how exact they have to be, the bound alone decides.
No kernel may reach another device: no remote copies, remote signals or barrier semaphores. Data moves between devices by JAX's collectives and lax.ppermute only.
A program may use at most 192 MiB of HBM per device.

v0:
```python
import jax
import jax.numpy as jnp
from jax import lax
from jax.sharding import PartitionSpec as P

NI = 512
NS = 512


def shifted(shard, axis, by):
    size = lax.axis_size(axis)
    return lax.ppermute(shard, axis, [(i, (i + by) % size) for i in range(size)])


def leaf_update(front_tile):
    interior = jnp.linalg.cholesky(front_tile[:NI, :NI])
    coupled = jax.scipy.linalg.solve_triangular(interior, front_tile[:NI, NI:], lower=True)
    return front_tile[NI:, NI:] - jnp.dot(coupled.T, coupled, precision=lax.Precision.HIGHEST)


def extend_add(update, placement):
    blocks_count = placement.shape[0]
    block_size = update.shape[0] // blocks_count
    joined_blocks = blocks_count + blocks_count // 2
    onehot = (placement[None, :] == jnp.arange(joined_blocks, dtype=jnp.int32)[:, None]).astype(
        jnp.float32
    )
    blocks = update.reshape(blocks_count, block_size, blocks_count, block_size)
    spread = jnp.einsum("ja,aibk,lb->jilk", onehot, blocks, onehot, precision=lax.Precision.HIGHEST)
    return spread.reshape(joined_blocks * block_size, joined_blocks * block_size)


def partial_factor(joined):
    corner = jnp.linalg.cholesky(joined[:NS, :NS])
    coupled = jax.scipy.linalg.solve_triangular(corner, joined[:NS, NS:], lower=True)
    factor_panel = jnp.concatenate([corner, coupled.T], axis=0)
    update = joined[NS:, NS:] - jnp.dot(coupled.T, coupled, precision=lax.Precision.HIGHEST)
    return (factor_panel, update)


def shards(leaf_front, place_pairs, place_quads):
    update_leaf = leaf_update(leaf_front)
    pair_row = place_pairs[0]
    quad_row = place_quads[0]
    half_cols = lax.axis_size("gx") // 2
    half_rows = lax.axis_size("gy") // 2
    other_update, other_place = shifted(
        (update_leaf, pair_row.astype(jnp.float32)), "gx", half_cols
    )
    joined_pair = extend_add(update_leaf, pair_row) + extend_add(
        other_update, other_place.astype(jnp.int32)
    )
    pair_panel, update_pair = partial_factor(joined_pair)
    partner_update, partner_place = shifted(
        (update_pair, quad_row.astype(jnp.float32)), "gy", half_rows
    )
    joined_quad = extend_add(update_pair, quad_row) + extend_add(
        partner_update, partner_place.astype(jnp.int32)
    )
    quad_panel, quad_update = partial_factor(joined_quad)
    return (pair_panel, quad_panel, quad_update)


def solution(mesh):
    in_specs = (P("gx", "gy"), P("gx", "gy"), P("gx", "gy"))
    out_specs = (P("gx", "gy"), P("gx", "gy"), P("gx", "gy"))
    return jax.shard_map(shards, mesh=mesh, in_specs=in_specs, out_specs=out_specs, check_vma=False)
```

profile of v0, /device:TPU:0, one launch (start us, length us, event | category | flops | bytes accessed | tf_op | source)
XLA Modules:
  0.0 862.9 jit_solution(18443791925368745812)
XLA Ops:
  3.7 11.7 %cholesky.374 = f32[128,128]{1,0:T(8,128)S(1)} custom-call(f32[128,128]{1,0:T(8,128)S(1)} %cholesky.586), custom_call_target="Cholesky" | custom-call | tf_op jit(solution)/shard_map/jit(cholesky)/cholesky | solution.py:16
  15.6 9.8 %custom-call.31 = f32[1,128,128]{1,2,0:T(8,128)S(1)} custom-call(f32[1,128,128]{2,1,0:T(8,128)S(1)} %get-tuple-element.97), custom_call_target="InvertDiagBlocksLowerTriangular" | custom-call | tf_op jit(solution)/shard_map/jit(cholesky)/cholesky | solution.py:16
  26.1 11.7 %cholesky.393 = f32[128,128]{1,0:T(8,128)S(1)} custom-call(f32[128,128]{1,0:T(8,128)S(1)} %cholesky.590), custom_call_target="Cholesky" | custom-call | tf_op jit(solution)/shard_map/jit(cholesky)/cholesky | solution.py:16
  37.9 10.0 %custom-call.32 = f32[1,128,128]{1,2,0:T(8,128)S(1)} custom-call(f32[1,128,128]{2,1,0:T(8,128)S(1)} %get-tuple-element.94), custom_call_target="InvertDiagBlocksLowerTriangular" | custom-call | tf_op jit(solution)/shard_map/jit(cholesky)/cholesky | solution.py:16
  48.5 11.7 %cholesky.414 = f32[128,128]{1,0:T(8,128)S(1)} custom-call(f32[128,128]{1,0:T(8,128)S(1)} %cholesky.595), custom_call_target="Cholesky" | custom-call | tf_op jit(solution)/shard_map/jit(cholesky)/cholesky | solution.py:16
  60.3 9.8 %custom-call.33 = f32[1,128,128]{1,2,0:T(8,128)S(1)} custom-call(f32[1,128,128]{2,1,0:T(8,128)S(1)} %get-tuple-element.91), custom_call_target="InvertDiagBlocksLowerTriangular" | custom-call | tf_op jit(solution)/shard_map/jit(cholesky)/cholesky | solution.py:16
  70.7 11.7 %cholesky.431 = f32[128,128]{1,0:T(8,128)S(1)} custom-call(f32[128,128]{1,0:T(8,128)S(1)} %convolution_subtract_fusion.14), custom_call_target="Cholesky" | custom-call | tf_op jit(solution)/shard_map/jit(cholesky)/cholesky | solution.py:16
  87.5 8.0 while.6
  95.6 39.3 %custom-call.34 = f32[4,128,128]{1,2,0:T(8,128)S(1)} custom-call(f32[4,128,128]{2,1,0:T(8,128)S(1)} %get-tuple-element.25), custom_call_target="InvertDiagBlocksLowerTriangular" | custom-call | tf_op jit(solution)/shard_map/jit(_solve_triangular)/triangular_solve | solution.py:17
  138.8 1.8 convolution_subtract_fusion.2
  141.2 2.2 fusion.51
  144.1 10.1 %slice_subtract_fusion.2 = f32[1024,1024]{1,0:T(8,128)} fusion(f32[1536,1536]{1,0:T(8,128)} %param.6, f32[128,1024]{1,0:T(8,128)S(1)} %fusion.112, f32[128,1024]{1,0:T(8,128)S(1)} %fusion.113, f32[128,1024]{1,0:T(8,128)S(1)} %fusion.115, f32[128,1024]{1,0:T(8,128)S(1)} %fusion.74), kind=kOutput, calls=%fused_computation.28 | convolution fusion | flops 6445072384 | bytes 10485760 | tf_op jit(solution)/shard_map/dot_general | solution.py:18
  154.1 4.1 collective-permute-start
  158.3 3.2 copy.46
  161.5 5.8 fusion.18
  167.3 6.8 fusion.6
  174.2 164.9 %collective-permute-done.1 = f32[8]{0:T(128)S(1)} collective-permute-done((f32[8]{0:T(128)S(1)}, f32[8]{0:T(128)S(1)}, u32[]{:S(2)}, u32[]{:S(2)}) %collective-permute-start.1) | collective-permute-done | bytes 64 | tf_op jit(solution)/shard_map/ppermute | solution.py:12
  339.0 3.2 copy.47
  342.2 6.9 fusion.16
  349.2 13.2 %add_bitcast_fusion.1 = f32[12,128,12,128]{3,2,0,1:T(8,128)} fusion(f32[128,128,12,12]{1,3,2,0:T(8,128)S(1)} %fusion.6, f32[128,8,128,12]{2,3,1,0:T(8,128)} %fusion.16, s32[8]{0:T(128)S(1)} %convert_element_type.17), kind=kOutput, calls=%fused_computation.7 | convolution fusion | flops 228851808 | bytes 25165856 | tf_op jit(solution)/shard_map/ja,aibk,lb->jilk/dot_general | solution.py:29
  362.3 10.3 %copy.21 = f32[12,128,12,128]{3,2,1,0:T(8,128)} copy(f32[12,128,12,128]{3,2,0,1:T(8,128)} %add_bitcast_fusion.1) | data formatting | bytes 18874368 | tf_op jit(solution)/shard_map/add | solution.py:50
  372.7 9.3 %copy.75 = f32[192,8,12,128]{3,1,2,0:T(8,128)S(1)} copy(f32[192,8,12,128]{3,2,1,0:T(8,128)} %bitcast.202) | data formatting | bytes 18874368
  382.0 3.6 copy-done.1
  387.5 11.7 %cholesky.446 = f32[128,128]{1,0:T(8,128)S(1)} custom-call(f32[128,128]{1,0:T(8,128)S(1)} %cholesky.599), custom_call_target="Cholesky" | custom-call | tf_op jit(solution)/shard_map/jit(cholesky)/cholesky | solution.py:34
  399.4 10.0 %custom-call.35 = f32[1,128,128]{1,2,0:T(8,128)S(1)} custom-call(f32[1,128,128]{2,1,0:T(8,128)S(1)} %get-tuple-element.87), custom_call_target="InvertDiagBlocksLowerTriangular" | custom-call | tf_op jit(solution)/shard_map/jit(cholesky)/cholesky | solution.py:34
  410.0 11.7 %cholesky.465 = f32[128,128]{1,0:T(8,128)S(1)} custom-call(f32[128,128]{1,0:T(8,128)S(1)} %cholesky.603), custom_call_target="Cholesky" | custom-call | tf_op jit(solution)/shard_map/jit(cholesky)/cholesky | solution.py:34
  421.7 9.8 %custom-call.36 = f32[1,128,128]{1,2,0:T(8,128)S(1)} custom-call(f32[1,128,128]{2,1,0:T(8,128)S(1)} %get-tuple-element.84), custom_call_target="InvertDiagBlocksLowerTriangular" | custom-call | tf_op jit(solution)/shard_map/jit(cholesky)/cholesky | solution.py:34
  432.2 11.7 %cholesky.486 = f32[128,128]{1,0:T(8,128)S(1)} custom-call(f32[128,128]{1,0:T(8,128)S(1)} %cholesky.608), custom_call_target="Cholesky" | custom-call | tf_op jit(solution)/shard_map/jit(cholesky)/cholesky | solution.py:34
  444.0 10.0 %custom-call.37 = f32[1,128,128]{1,2,0:T(8,128)S(1)} custom-call(f32[1,128,128]{2,1,0:T(8,128)S(1)} %get-tuple-element.81), custom_call_target="InvertDiagBlocksLowerTriangular" | custom-call | tf_op jit(solution)/shard_map/jit(cholesky)/cholesky | solution.py:34
  454.6 11.7 %cholesky.503 = f32[128,128]{1,0:T(8,128)S(1)} custom-call(f32[128,128]{1,0:T(8,128)S(1)} %convolution_subtract_fusion.13), custom_call_target="Cholesky" | custom-call | tf_op jit(solution)/shard_map/jit(cholesky)/cholesky | solution.py:34
  471.9 8.0 while.7
  479.9 39.7 %custom-call.38 = f32[4,128,128]{1,2,0:T(8,128)S(1)} custom-call(f32[4,128,128]{2,1,0:T(8,128)S(1)} %get-tuple-element.26), custom_call_target="InvertDiagBlocksLowerTriangular" | custom-call | tf_op jit(solution)/shard_map/jit(_solve_triangular)/triangular_solve | solution.py:35
  526.0 2.3 fusion.48
  528.9 9.8 %slice_subtract_fusion.1 = f32[1024,1024]{1,0:T(8,128)} fusion(f32[1536,1536]{1,0:T(8,128)} %bitcast.219, f32[128,1024]{1,0:T(8,128)S(1)} %fusion.106, f32[128,1024]{1,0:T(8,128)S(1)} %fusion.107, f32[128,1024]{1,0:T(8,128)S(1)} %fusion.109, f32[128,1024]{1,0:T(8,128)S(1)} %fusion.72), kind=kOutput, calls=%fused_computation.19 | convolution fusion | flops 6445072384 | bytes 10485760 | tf_op jit(solution)/shard_map/dot_general | solution.py:37
  540.8 90.1 %collective-permute-done.3 = f32[8]{0:T(128)S(1)} collective-permute-done((f32[8]{0:T(128)S(1)}, f32[8]{0:T(128)S(1)}, u32[]{:S(2)}, u32[]{:S(2)}) %collective-permute-start.3) | collective-permute-done | bytes 64 | tf_op jit(solution)/shard_map/ppermute | solution.py:12
  633.7 2.5 copy.29
  636.2 3.2 copy.49
  639.4 5.8 fusion.14
  645.2 6.8 fusion.2
  652.0 3.2 copy.50
  655.2 6.9 fusion.12
  662.1 13.2 %add_bitcast_fusion = f32[12,128,12,128]{3,2,0,1:T(8,128)} fusion(f32[128,128,12,12]{1,3,2,0:T(8,128)S(1)} %fusion.2, f32[128,8,128,12]{2,3,1,0:T(8,128)} %fusion.12, s32[8]{0:T(128)S(1)} %convert_element_type.19), kind=kOutput, calls=%fused_computation.6 | convolution fusion | flops 228851808 | bytes 25165856 | tf_op jit(solution)/shard_map/ja,aibk,lb->jilk/dot_general | solution.py:29
  675.3 10.3 %copy.25 = f32[12,128,12,128]{3,2,1,0:T(8,128)} copy(f32[12,128,12,128]{3,2,0,1:T(8,128)} %add_bitcast_fusion) | data formatting | bytes 18874368 | tf_op jit(solution)/shard_map/add | solution.py:57
  685.7 9.3 %copy.74 = f32[192,8,12,128]{3,1,2,0:T(8,128)S(1)} copy(f32[192,8,12,128]{3,2,1,0:T(8,128)} %bitcast.203) | data formatting | bytes 18874368
  694.9 3.6 copy-done
  700.4 11.7 %cholesky.518 = f32[128,128]{1,0:T(8,128)S(1)} custom-call(f32[128,128]{1,0:T(8,128)S(1)} %cholesky.612), custom_call_target="Cholesky" | custom-call | tf_op jit(solution)/shard_map/jit(cholesky)/cholesky | solution.py:34
  712.3 10.0 %custom-call.39 = f32[1,128,128]{1,2,0:T(8,128)S(1)} custom-call(f32[1,128,128]{2,1,0:T(8,128)S(1)} %get-tuple-element.77), custom_call_target="InvertDiagBlocksLowerTriangular" | custom-call | tf_op jit(solution)/shard_map/jit(cholesky)/cholesky | solution.py:34
  723.0 11.7 %cholesky.537 = f32[128,128]{1,0:T(8,128)S(1)} custom-call(f32[128,128]{1,0:T(8,128)S(1)} %cholesky.616), custom_call_target="Cholesky" | custom-call | tf_op jit(solution)/shard_map/jit(cholesky)/cholesky | solution.py:34
  734.7 9.8 %custom-call.40 = f32[1,128,128]{1,2,0:T(8,128)S(1)} custom-call(f32[1,128,128]{2,1,0:T(8,128)S(1)} %get-tuple-element.74), custom_call_target="InvertDiagBlocksLowerTriangular" | custom-call | tf_op jit(solution)/shard_map/jit(cholesky)/cholesky | solution.py:34
  745.2 11.7 %cholesky.558 = f32[128,128]{1,0:T(8,128)S(1)} custom-call(f32[128,128]{1,0:T(8,128)S(1)} %cholesky.621), custom_call_target="Cholesky" | custom-call | tf_op jit(solution)/shard_map/jit(cholesky)/cholesky | solution.py:34
  756.9 10.0 %custom-call.41 = f32[1,128,128]{1,2,0:T(8,128)S(1)} custom-call(f32[1,128,128]{2,1,0:T(8,128)S(1)} %get-tuple-element.71), custom_call_target="InvertDiagBlocksLowerTriangular" | custom-call | tf_op jit(solution)/shard_map/jit(cholesky)/cholesky | solution.py:34
  767.5 11.7 %cholesky.575 = f32[128,128]{1,0:T(8,128)S(1)} custom-call(f32[128,128]{1,0:T(8,128)S(1)} %convolution_subtract_fusion.12), custom_call_target="Cholesky" | custom-call | tf_op jit(solution)/shard_map/jit(cholesky)/cholesky | solution.py:34
  785.8 11.7 %while.8 = (s32[]{:T(128)}, f32[512,512]{1,0:T(8,128)}, s32[4,2]{0,1:T(2,128)S(1)}, f32[4,128,128]{2,1,0:T(8,128)S(1)}, s32[]{:T(128)}) while((s32[]{:T(128)}, f32[512,512]{1,0:T(8,128)}, s32[4,2]{0,1:T(2,128)S(1)}, f32[4,128,128]{2,1,0:T(8,128)S(1)}, s32[]{:T(128)}) %tuple.90), condition=%wide.while_cond.clone.1, body=%wide.while_body.clone.1.sunk | while | flops 2 | bytes 131189 | solution.py:35
  786.5 2.3 bitcast_dynamic-update-slice_fusion.8
  789.4 2.3 bitcast_dynamic-update-slice_fusion.8
  792.3 2.3 bitcast_dynamic-update-slice_fusion.8
  795.3 2.2 bitcast_dynamic-update-slice_fusion.8
  797.5 39.6 %custom-call.42 = f32[4,128,128]{1,2,0:T(8,128)S(1)} custom-call(f32[4,128,128]{2,1,0:T(8,128)S(1)} %get-tuple-element.27), custom_call_target="InvertDiagBlocksLowerTriangular" | custom-call | tf_op jit(solution)/shard_map/jit(_solve_triangular)/triangular_solve | solution.py:35
  837.1 1.8 fusion.70
  841.2 1.8 convolution_subtract_fusion
  843.7 2.4 fusion.45
  848.3 8.4 slice_subtract_fusion
  858.1 2.1 pad_maximum_fusion.1
  860.1 2.4 copy.30
  (148 shorter events, 64.6 us)
Async XLA Ops:
  144.0 14.2 %copy-start.4 = (s32[1,8]{1,0:T(1,128)S(1)}, s32[1,8]{1,0:T(1,128)}, u32[]{:S(2)}) copy-start(s32[1,8]{1,0:T(1,128)} %param.7) | copy-start | bytes 100
  154.1 184.9 %collective-permute-start = (f32[1024,1024]{1,0:T(8,128)}, f32[1024,1024]{1,0:T(8,128)}, u32[]{:S(2)}, u32[]{:S(2)}) collective-permute-start(f32[1024,1024]{1,0:T(8,128)} %slice_subtract_fusion.2), channel_id=1, source_target_pairs={{0,16},{8,24},{16,0},{24,8},{1,17},{9,25},{17,1},{25,9},{2,18},{10... | collective-permute-start | bytes 12582920 | tf_op jit(solution)/shard_map/ppermute | solution.py:12
  158.2 180.8 %collective-permute-start.1 = (f32[8]{0:T(128)S(1)}, f32[8]{0:T(128)S(1)}, u32[]{:S(2)}, u32[]{:S(2)}) collective-permute-start(f32[8]{0:T(128)S(1)} %bitcast_convert_fusion.1), channel_id=1, source_target_pairs={{0,16},{8,24},{16,0},{24,8},{1,17},{9,25},{17,1},{25,9},{2,18},{10... | collective-permute-start | bytes 104 | tf_op jit(solution)/shard_map/ppermute | solution.py:12
  382.0 3.6 copy-start.1
  479.9 43.7 %copy-start.3 = (f32[512,512]{1,0:T(8,128)}, f32[512,512]{1,0:T(8,128)S(1)}, u32[]{:S(2)}) copy-start(f32[512,512]{1,0:T(8,128)S(1)} %get-tuple-element.240) | copy-start | bytes 3145732
  528.9 11.4 %copy-start.5 = (s32[1,8]{1,0:T(1,128)S(1)}, s32[1,8]{1,0:T(1,128)}, u32[]{:S(2)}) copy-start(s32[1,8]{1,0:T(1,128)} %param.8) | copy-start | bytes 100
  538.8 113.2 %collective-permute-start.2 = (f32[1024,1024]{1,0:T(8,128)}, f32[1024,1024]{1,0:T(8,128)}, u32[]{:S(2)}, u32[]{:S(2)}) collective-permute-start(f32[1024,1024]{1,0:T(8,128)} %slice_subtract_fusion.1), channel_id=1, source_target_pairs={{0,4},{1,5},{2,6},{3,7},{4,0},{5,1},{6,2},{7,3},{8,12},{9,13},{10,... | collective-permute-start | bytes 12582920 | tf_op jit(solution)/shard_map/ppermute | solution.py:12
  540.3 90.5 %collective-permute-start.3 = (f32[8]{0:T(128)S(1)}, f32[8]{0:T(128)S(1)}, u32[]{:S(2)}, u32[]{:S(2)}) collective-permute-start(f32[8]{0:T(128)S(1)} %bitcast_convert_fusion), channel_id=1, source_target_pairs={{0,4},{1,5},{2,6},{3,7},{4,0},{5,1},{6,2},{7,3},{8,12},{9,13},{10,... | collective-permute-start | bytes 104 | tf_op jit(solution)/shard_map/ppermute | solution.py:12
  632.2 1.2 copy-start.2
  694.9 3.6 copy-start
  744.5 103.8 %slice-start = ((s8[9437184]{0:T(1024)(128)(4,1)}), s8[1048576]{0:T(1024)(128)(4,1)S(1)}, s32[]{:S(2)}) async-start(s8[9437184]{0:T(1024)(128)(4,1)} %bitcast.210), calls=%async_computation | async-start | bytes 2097152
  837.1 11.3 %slice-start.1 = ((s8[9437184]{0:T(1024)(128)(4,1)}), s8[4194304]{0:T(1024)(128)(4,1)S(1)}, s32[]{:S(2)}) async-start(s8[9437184]{0:T(1024)(128)(4,1)} %bitcast.210), calls=%async_computation.1 | async-start | bytes 8388608
  843.7 4.6 slice-start.2
where the time goes:
time: 873 us; the launch traced here: 863 us
  other arithmetic  366 us (42%)
  waiting for transfers between devices  255 us (29%)
  matrix products  127 us (15%)
  local copies, waits for them, and re-layouts  98.2 us (11%)
  between operations  9.61 us (1%)
    ppermute x4, waiting for transfers between devices, shifted(): lax.ppermute(shard, axis, [(i, (i + by) % size) for i in range(size)])  255 us
    another operation x30, other arithmetic, partial_factor(): corner = jnp.linalg.cholesky(joined[:NS, :NS])  159 us
    another operation x4, other arithmetic, partial_factor(): jax.scipy.linalg.solve_triangular(corner, joined[:NS, NS:], lower=True)  80.8 us
    another operation x14, other arithmetic, leaf_update(): interior = jnp.linalg.cholesky(front_tile[:NI, :NI])  78.6 us
    dot_general x8, matrix products, extend_add(): jnp.einsum('ja,aibk,lb->jilk', onehot, blocks, onehot, precision=lax.Prec...  65.4 us
    unnamed x29, local copies, waits for them, and re-layouts  45.6 us
    another operation x3, other arithmetic, leaf_update(): jax.scipy.linalg.solve_triangular(interior, front_tile[:NI, NI:], lower=T...  39.8 us
    another operation x24, local copies, waits for them, and re-layouts, partial_factor(): jax.scipy.linalg.solve_triangular(corner, joined[:NS, NS:], lower=True)  19.5 us
  transfers between devices with their start and end apart: 4, of which 2 were waited for; matrix products, arithmetic and copies ran while one was open for 4% of the time, Pallas kernels for 0%

commit v1 on v0

v1 whole, which is shorter than its diff:
```python
import jax
import jax.numpy as jnp
from jax import lax
from jax.experimental import pallas as pl
from jax.experimental.pallas import tpu as pltpu
from jax.sharding import PartitionSpec as P

f32 = jnp.float32
bf16 = jnp.bfloat16
NT = (((1,), (1,)), ((), ()))
TN = (((0,), (0,)), ((), ()))
BLK = 128
KB = 8
KS = 4
NS = KS * BLK
NB = KB * BLK
NJ = NS + NB
LOWER = [(a, b) for a in range(KS) for b in range(a + 1)]
VMEM = pl.BlockSpec(memory_space=pltpu.VMEM)
SMEM = pl.BlockSpec(memory_space=pltpu.SMEM)
HBM = pl.BlockSpec(memory_space=pltpu.HBM)


def sds(*shape):
    return jax.ShapeDtypeStruct(shape, f32)


def call(body, out, ins, outs, scratch, args, vmem=32):
    return pl.pallas_call(
        body,
        out_shape=out,
        in_specs=ins,
        out_specs=outs,
        scratch_shapes=scratch,
        cost_estimate=pl.CostEstimate(flops=1000, bytes_accessed=1000, transcendentals=0),
        compiler_params=pltpu.CompilerParams(vmem_limit_bytes=vmem * 1024 * 1024),
    )(*args)


def split(x):
    hi = x.astype(bf16)
    return hi, (x - hi.astype(f32)).astype(bf16)


def dot(a, b, dims):
    return lax.dot_general(a, b, dims, preferred_element_type=f32)


def mm3(a, b):
    return dot(jnp.concatenate([a[0], a[0], a[1]], 1), jnp.concatenate([b[0], b[1], b[0]], 1), NT)


def row(x, k):
    return jnp.broadcast_to(x[k : k + 1, :], x.shape)


def col(x, j):
    return jnp.broadcast_to(x[:, j : j + 1], (8, BLK))


def factor_block(block):
    ri = lax.broadcasted_iota(jnp.int32, (8, BLK), 0)
    ci = lax.broadcasted_iota(jnp.int32, (8, BLK), 1)
    count, wide = BLK // 8, 4
    left = [block[8 * t : 8 * t + 8, :] for t in range(count)]
    right = [jnp.where(ci == ri + 8 * t, 1.0, 0.0).astype(f32) for t in range(count)]
    upper, inverse = [], []
    here = [col(left[0], k) for k in range(8)]
    for s in range(count):
        end = (s // wide + 1) * wide
        ahead = {w: [col(left[w], 8 * s + k) for k in range(8)] for w in range(s + 1, min(end + 1, count))}
        following = [col(left[s + 1], 8 * s + 8 + k) for k in range(8)] if s + 1 < count else None
        a, t = left[s], right[s]
        pivots = None
        for k in range(8):
            pivot = row(here[k], k)
            inv = pl.reciprocal(pivot, approx=True)
            pivots = pivot if k == 0 else jnp.where(ri == k, pivot, pivots)
            mult = jnp.where(ri > k, here[k], 0.0) * inv
            rows = {m: row(here[m], k) for m in range(k + 1, 8)}
            row_a, row_t = row(a, k), row(t, k)
            for m in range(k + 1, 8):
                here[m] = here[m] - mult * rows[m]
            a = a - mult * row_a
            t = t - mult * row_t
            for w, cols in ahead.items():
                mult = cols[k] * inv
                if w == s + 1:
                    following = [f - mult * row(cols[k], m) for m, f in enumerate(following)]
                for m in range(k + 1, 8):
                    cols[m] = cols[m] - mult * rows[m]
                left[w] = left[w] - mult * row_a
                right[w] = right[w] - mult * row_t
        here = following
        scale = lax.rsqrt(pivots)
        upper.append(a * scale)
        inverse.append(t * scale)
        if s + 1 == end and end + 1 < count:
            ah, al = split(jnp.concatenate(upper[-wide:], 0))
            th, tl = split(jnp.concatenate(inverse[-wide:], 0))
            lhs = jnp.concatenate([ah, ah, al], 0)
            rhs_a = jnp.concatenate([ah, al, ah], 0)
            rhs_t = jnp.concatenate([th, tl, th], 0)
            outer = dot(lhs, jnp.concatenate([rhs_a, rhs_t], 1), TN)
            for q in range(end + 1, count):
                left[q] = left[q] - outer[8 * q : 8 * q + 8, :BLK]
                right[q] = right[q] - outer[8 * q : 8 * q + 8, BLK:]
    return jnp.concatenate(inverse, 0)


def factor(work, x, lower, inv, corner):
    ri = lax.broadcasted_iota(jnp.int32, (NS, BLK), 0)
    ci = lax.broadcasted_iota(jnp.int32, (NS, BLK), 1)

    def finish(k, inverse):
        here = at(BLK * k)
        inv[k] = inverse
        lower[:, here] = jnp.where(ri >= ci + BLK * k, mm3(split(work[:, here]), split(inverse)), 0.0)
        if not isinstance(k, int) or k + 1 < KS:
            then = at(BLK * jnp.minimum(k + 1, KS - 1))
            pair = split(lower[then, here])
            corner[...] = work[then, then] - mm3(pair, pair)

    def update(k):
        here = at(BLK * k)
        pair = split(lower[:, here])
        work[...] = work[...] - mm3(pair, pair)
        done = mm3(split(x[:, here]), split(inv[k]))
        x[...] = x[...] - mm3(split(done), pair)
        x[:, here] = done

    def step(k, carry):
        inverse = factor_block(corner[...])
        update(k - 1)
        finish(k, inverse)
        return carry

    finish(0, factor_block(work[0:BLK, 0:BLK]))
    lax.fori_loop(1, KS, step, 0)
    x[:, NS - BLK :] = mm3(split(x[:, NS - BLK :]), split(inv[KS - 1]))


def solve(x, lower, inv):
    for k in range(KS):
        o, e = BLK * k, BLK * (k + 1)
        done = mm3(split(x[:, o:e]), split(inv[k]))
        x[:, o:e] = done
        if k + 1 < KS:
            x[:, e:] = x[:, e:] - mm3(split(done), split(lower[e:, o:e]))


def ranks(values):
    out = []
    for a, va in enumerate(values):
        r = jnp.int32(0)
        for b, vb in enumerate(values):
            if a != b:
                r = r + (vb < va).astype(jnp.int32)
        out.append(r)
    return out


def sort_blocks(place, order):
    values = [place[0, a] for a in range(KB)]
    for a, r in enumerate(ranks(values)):
        order[r] = jnp.int32(a)


def at(start):
    return pl.ds(pl.multiple_of(start, BLK), BLK)


def leaf_a(front, place, corner, w_out, a, lower, inv, next_block, ss, order, sems):
    sort_blocks(place, order)
    copies = [pltpu.make_async_copy(front.at[0:NS, 0:NS], a, sems.at[0])]
    copies[0].start()
    for t in range(KB):
        c = pltpu.make_async_copy(
            front.at[at(NS + BLK * order[t]), 0:NS], w_out.at[BLK * t : BLK * t + BLK, :], sems.at[1 + t]
        )
        c.start()
        copies.append(c)
    for n, (i, j) in enumerate(LOWER):
        c = pltpu.make_async_copy(
            front.at[at(NS + BLK * order[i]), at(NS + BLK * order[j])], ss.at[n], sems.at[1 + KB + n]
        )
        c.start()
        copies.append(c)
    for c in copies:
        c.wait()
    factor(a, w_out, lower, inv, next_block)
    w = split(w_out[0:NS, :])
    for i in range(KS):
        rows = slice(BLK * i, BLK * i + BLK)
        left = tuple(v[rows] for v in w)
        right = tuple(v[: BLK * i + BLK] for v in w)
        gram = mm3(left, right)
        for j in range(i + 1):
            n = LOWER.index((i, j))
            corner[n] = ss[n] - gram[:, BLK * j : BLK * j + BLK]


def leaf_b(front, place, w, rs, rs_a, rs_b, rr_low, f_rs, f_rr, order, sems):
    sort_blocks(place, order)
    copies = []
    for i in range(KS):
        for j in range(KB):
            dst = f_rs if j < KS else f_rr
            c = pltpu.make_async_copy(
                front.at[at(NS + BLK * order[KS + i]), at(NS + BLK * order[j])],
                dst.at[BLK * i : BLK * i + BLK, BLK * (j % KS) : BLK * (j % KS) + BLK],
                sems.at[i * KB + j],
            )
            c.start()
            copies.append(c)
    ws, wr = split(w[0:NS, :]), split(w[NS:, :])
    g_rs = mm3(wr, ws)
    g_rr = mm3(wr, wr)
    for c in copies:
        c.wait()
    rs[...] = f_rs[...] - g_rs
    rs_a[...] = rs[: NS // 2, :]
    rs_b[...] = rs[NS // 2 :, :]
    rr = f_rr[...] - g_rr
    for n, (i, j) in enumerate(LOWER):
        rr_low[n] = rr[BLK * i : BLK * i + BLK, BLK * j : BLK * j + BLK]


def merge_a(mine, other, rs, lower, inv, v, work, next_block):
    for n, (i, j) in enumerate(LOWER):
        block = mine[n] + other[n]
        work[BLK * i : BLK * i + BLK, BLK * j : BLK * j + BLK] = block
        if i != j:
            work[BLK * j : BLK * j + BLK, BLK * i : BLK * i + BLK] = block.T
    v[...] = rs[...]
    factor(work, v, lower, inv, next_block)


def canonical(info, order):
    places = []
    for r in range(2):
        row_of = info.at[r : r + 1]
        sort_blocks(row_of, order)
        places += [row_of[0, order[KS + i]] for i in range(KS)]
    return [info[2, p - KS] for p in places]


def corner_blocks(low):
    blocks = {}
    for n, (i, j) in enumerate(LOWER):
        blocks[i, j] = low[n]
        if i != j:
            blocks[j, i] = low[n].T
    return blocks


def row_blocks(*parts):
    return [v.at[o : o + BLK, :] for v in parts for o in range(0, v.shape[0], BLK)]


def pair_update(rows, rr_low, spots, update, vs):
    where = ranks(spots)
    for e in range(KB):
        vs[at(BLK * where[e]), :] = rows[e][...]
    top, low = split(vs[0:NS, :]), split(vs[NS:, :])
    update[0:NS, 0:NS] = -mm3(top, top)
    update[NS:, 0:NS] = -mm3(low, top)
    update[NS:, NS:] = -mm3(low, low)
    for (i, j), block in corner_blocks(rr_low).items():
        r, c = at(BLK * where[i]), at(BLK * where[j])
        update[r, c] = update[r, c] + block


def merge_b(lower, inv, rs_other, v):
    v[...] = rs_other[...]
    solve(v, lower, inv)


def assemble_mine(lower, v_mine, v_first, v_second, rr_low, info, panel, update, vs, order):
    rows = row_blocks(v_mine, v_first, v_second)
    pair_update(rows, rr_low, canonical(info, order), update, vs)
    panel[0:NS, :] = lower[...]
    for r in range(2):
        row_of = info.at[r : r + 1]
        sort_blocks(row_of, order)
        for i in range(KS):
            panel[at(BLK * row_of[0, order[KS + i]]), :] = rows[KS * r + i][...]


def assemble_other(v_mine, v_first, v_second, rr_low, info, update, vs, order):
    pair_update(row_blocks(v_mine, v_first, v_second), rr_low, canonical(info, order), update, vs)


def last(up_a, up_b, low_a, low_b, info_a, info_b, panel, update, work, x, lower, inv, next_block, buf, order, sems):
    pairs = []
    for up, low, info in ((up_a, low_a, info_a), (up_b, low_b, info_b)):
        spots = canonical(info, order)
        pairs.append((up, corner_blocks(low), spots, ranks(spots)))
    work[...] = up_a[0:NS, 0:NS] + up_b[0:NS, 0:NS]
    for up, blocks, spots, where in pairs:
        for e in range(KB):

            @pl.when(where[e] >= KS)
            def _():
                x[at(BLK * (spots[e] - KS)), :] = up[at(BLK * where[e]), 0:NS]

        for (i, j), block in blocks.items():
            si, sj = spots[KS + i], spots[KS + j]

            @pl.when((si < KS) & (sj < KS))
            def _():
                r, c = at(BLK * si), at(BLK * sj)
                work[r, c] = work[r, c] + block

            @pl.when((si >= KS) & (sj < KS))
            def _():
                r, c = at(BLK * (si - KS)), at(BLK * sj)
                x[r, c] = x[r, c] + block

    factor(work, x, lower, inv, next_block)
    outs = [
        pltpu.make_async_copy(lower, panel.at[0:NS, :], sems.at[0]),
        pltpu.make_async_copy(x, panel.at[NS:, :], sems.at[1]),
    ]
    for c in outs:
        c.start()
    pair = split(x[...])
    for t in range(KB):
        rows = slice(BLK * t, BLK * t + BLK)
        buf[rows, :] = -mm3(tuple(p[rows] for p in pair), pair)
    for up, blocks, spots, where in pairs:
        for e in range(KB):
            for f in range(KB):

                @pl.when((where[e] >= KS) & (where[f] >= KS))
                def _():
                    r, c = at(BLK * (spots[e] - KS)), at(BLK * (spots[f] - KS))
                    add = up[at(BLK * where[e]), at(BLK * where[f])]
                    if e >= KS and f >= KS:
                        add = add + blocks[e - KS, f - KS]
                    buf[r, c] = buf[r, c] + add

    c = pltpu.make_async_copy(buf, update, sems.at[2])
    c.start()
    outs.append(c)
    for c in outs:
        c.wait()


def after(x, *earlier):
    return lax.optimization_barrier((x,) + earlier)[0]


def shards(leaf_front, place_pairs, place_quads):
    dma = pltpu.SemaphoreType.DMA
    tri = len(LOWER)
    half_cols = lax.axis_size("gx") // 2
    half_rows = lax.axis_size("gy") // 2

    def partner(x, axis):
        half = half_cols if axis == "gx" else half_rows
        return lax.ppermute(x, axis, [(i, (i + half) % (2 * half)) for i in range(2 * half)])

    pairs_other = partner(place_pairs, "gx")
    order = pltpu.SMEM((KB,), jnp.int32)

    corner, w = call(
        leaf_a, (sds(tri, BLK, BLK), sds(NB, NS)), [HBM, SMEM], [VMEM, VMEM],
        [pltpu.VMEM((NS, NS), f32), pltpu.VMEM((NS, NS), f32), pltpu.VMEM((KS, BLK, BLK), f32), pltpu.VMEM((BLK, BLK), f32),
         pltpu.VMEM((tri, BLK, BLK), f32), order, dma((1 + KB + tri,))],
        (leaf_front, place_pairs), 52)
    corner_other = partner(after(corner, pairs_other), "gx")
    half = NS // 2
    rs, rs_a, rs_b, rr_low = call(
        leaf_b, (sds(NS, NS), sds(half, NS), sds(half, NS), sds(tri, BLK, BLK)), [HBM, SMEM, VMEM], [VMEM] * 4,
        [pltpu.VMEM((NS, NS), f32), pltpu.VMEM((NS, NS), f32), order, dma((KS * KB,))],
        (leaf_front, place_pairs, w), 52)
    rr_far = partner(rr_low, "gy")
    info = jnp.concatenate([place_pairs, pairs_other, place_quads], 0)
    info_other = partner(info, "gy")
    corner, info_other = lax.optimization_barrier((corner, info_other))
    rs_first = partner(after(rs_a, corner_other), "gx")

    lower, inv, v_mine = call(
        merge_a, (sds(NS, NS), sds(KS, BLK, BLK), sds(NS, NS)), [VMEM] * 3, [VMEM] * 3,
        [pltpu.VMEM((NS, NS), f32), pltpu.VMEM((BLK, BLK), f32)], (corner, corner_other, rs))
    v_mine_far = partner(v_mine, "gy")
    rs_second = partner(after(rs_b, rs_first, lower, rr_far), "gx")
    v_first = call(merge_b, sds(half, NS), [VMEM] * 3, VMEM, [], (lower, inv, rs_first))
    v_first_far = partner(v_first, "gy")
    rr_other = partner(after(rr_low, rs_second, v_mine_far, v_first), "gx")
    v_second = call(merge_b, sds(half, NS), [VMEM] * 3, VMEM, [], (lower, inv, rs_second))
    v_second_far = partner(v_second, "gy")
    scratch = [pltpu.VMEM((NB, NS), f32), order]
    pair_panel, update = call(
        assemble_mine, (sds(NS + NB, NS), sds(NB, NB)), [VMEM] * 5 + [SMEM], [VMEM] * 2, scratch,
        (lower, v_mine, v_first, v_second, rr_low, info))
    rr_other_far = partner(after(rr_other, update, v_first_far, v_second_far), "gy")
    update_far = call(
        assemble_other, sds(NB, NB), [VMEM] * 4 + [SMEM], VMEM, scratch,
        (v_mine_far, v_first_far, v_second_far, rr_far, info_other))
    quad_panel, quad_update = call(
        last, (sds(NS + NB, NS), sds(NB, NB)), [VMEM] * 4 + [SMEM] * 2, [HBM, HBM],
        [pltpu.VMEM((NS, NS), f32), pltpu.VMEM((NB, NS), f32), pltpu.VMEM((NS, NS), f32),
         pltpu.VMEM((KS, BLK, BLK), f32), pltpu.VMEM((BLK, BLK), f32), pltpu.VMEM((NB, NB), f32), order, dma((3,))],
        (update, update_far, rr_other, rr_other_far, info, info_other))
    return pair_panel, quad_panel, quad_update


def solution(mesh):
    spec = P("gx", "gy")
    return jax.shard_map(
        shards, mesh=mesh, in_specs=(spec, spec, spec), out_specs=(spec, spec, spec), check_vma=False
    )
```

time: 873 us -> 180 us (0.21); the launches traced: 863 us -> 180 us
  other arithmetic: 366 us -> 0.01 us
  waiting for transfers between devices: 255 us -> 89.7 us
  matrix products: 127 us -> 0 us
  local copies, waits for them, and re-layouts: 98.2 us -> 1.92 us
  Pallas kernels: 0 us -> 76.1 us
    another operation x51 -> x0, other arithmetic: 358 us -> none  [the longest x30 159 us: partial_factor(): corner = jnp.linalg.cholesky(joined[:NS, :NS])]
    ppermute x4 -> x11, waiting for transfers between devices: 255 us -> 89.7 us  [partner(): lax.ppermute(x, axis, [(i, (i + half) % (2 * half)) for i in range(2 * ha...]
    dot_general x11 -> x0, matrix products: 93.7 us -> none  [the longest x8 65.4 us: extend_add(): jnp.einsum('ja,aibk,lb->jilk', onehot, blocks, onehot, precision=lax.Prec...]
    pallas_call x0 -> x8, Pallas kernels: none -> 76.1 us  [call(): pl.pallas_call(body, out_shape=out, in_specs=ins, out_specs=outs, scratch...]
    unnamed x29 -> x6, local copies, waits for them, and re-layouts: 45.6 us -> 1.92 us
    another operation x39 -> x0, matrix products: 33.5 us -> none  [the longest x14 18.8 us: partial_factor(): jax.scipy.linalg.solve_triangular(corner, joined[:NS, NS:], lower=True)]
    another operation x52 -> x0, local copies, waits for them, and re-layouts: 27.9 us -> none  [the longest x24 19.5 us: partial_factor(): jax.scipy.linalg.solve_triangular(corner, joined[:NS, NS:], lower=True)]
    add x2 -> x0, local copies, waits for them, and re-layouts: 20.7 us -> none  [the longest x1 10.3 us: shards(): extend_add(update_leaf, pair_row)]
  transfers between devices with their start and end apart: 4 -> 11, of which waited for: 2 -> 7; matrix products, arithmetic and copies ran while one was open for 4% -> 0% of each run, Pallas kernels for 0% -> 27%
where the time goes in v1:
time: 180 us
  waiting for transfers between devices  89.7 us (50%)
  Pallas kernels  76.1 us (42%)
  starting transfers between devices  11.5 us (6%)
  local copies, waits for them, and re-layouts  1.92 us (1%)
    ppermute x11, waiting for transfers between devices, partner(): lax.ppermute(x, axis, [(i, (i + half) % (2 * half)) for i in range(2 * ha...  89.7 us
    pallas_call x8, Pallas kernels, call(): pl.pallas_call(body, out_shape=out, in_specs=ins, out_specs=outs, scratch...  76.1 us
    ppermute x11, starting transfers between devices, partner(): lax.ppermute(x, axis, [(i, (i + half) % (2 * half)) for i in range(2 * ha...  11.5 us
  transfers between devices with their start and end apart: 11, of which 7 were waited for; matrix products, arithmetic and copies ran while one was open for 0% of the time, Pallas kernels for 27%

profile of v1, /device:TPU:0, one launch (start us, length us, event | category | flops | bytes accessed | tf_op | source)
XLA Modules:
  0.0 180.2 jit_solution(10837423546376533015)
XLA Ops:
  0.6 4.1 %collective-permute-start = (s32[1,8]{1,0:T(1,128)}, s32[1,8]{1,0:T(1,128)S(1)}, u32[]{:S(2)}, u32[]{:S(2)}) collective-permute-start(s32[1,8]{1,0:T(1,128)} %place.3), channel_id=1, source_target_pairs={{0,16},{8,24},{16,0},{24,8},{1,17},{9,25},{17,1},{25,9},{2,18},{10... | collective-permute-start | bytes 104 | tf_op jit(solution)/shard_map/ppermute | solution.py:362
  4.7 0.0 copy-start.1
  4.7 0.7 copy-done.1
  5.4 18.6 %shard_map.58 = (f32[10,128,128]{2,1,0:T(8,128)S(1)}, f32[1024,512]{1,0:T(8,128)}) custom-call(f32[1536,1536]{1,0:T(8,128)} %front.3, s32[1,8]{1,0:T(1,128)S(1)} %copy-done.1), custom_call_target="tpu_custom_call" | custom-call | flops 1000 | bytes 1000 | tf_op jit(solution)/shard_map/pallas_call | solution.py:29
  24.0 0.0 collective-permute-done
  24.0 0.1 collective-permute-start.2
  24.1 0.0 copy-start.2
  24.1 4.9 %shard_map.59 = (f32[512,512]{1,0:T(8,128)}, f32[256,512]{1,0:T(8,128)S(1)}, f32[256,512]{1,0:T(8,128)S(1)}, f32[10,128,128]{2,1,0:T(8,128)S(1)}) custom-call(f32[1536,1536]{1,0:T(8,128)} %front.3, s32[1,8]{1,0:T(1,128)S(1)} %copy-done.1, f32[1024,512]{1,0:T(8,128)} %get-tuple-element.26.w), custom_call_target="tpu_custom_call" | custom-call | flops 1000 | bytes 1000 | tf_op jit(solution)/shard_map/pallas_call | solution.py:29
  29.0 1.9 %collective-permute-start.4 = (f32[10,128,128]{2,1,0:T(8,128)S(1)}, f32[10,128,128]{2,1,0:T(8,128)S(1)}, u32[]{:S(2)}, u32[]{:S(2)}) collective-permute-start(f32[10,128,128]{2,1,0:T(8,128)S(1)} %get-tuple-element.39.rr_low), channel_id=1, source_target_pairs={{0,4},{1,5},{2,6},{3,7},{4,0},{5,1},{6,2},{7,3},{8,12},{9,13},{10,... | collective-permute-start | bytes 1966088 | tf_op jit(solution)/shard_map/ppermute | solution.py:362
  30.9 0.0 copy-done.2
  30.9 0.3 collective-permute-start.1
  31.2 24.0 %collective-permute-done.2.other = f32[10,128,128]{2,1,0:T(8,128)S(1)} collective-permute-done((f32[10,128,128]{2,1,0:T(8,128)S(1)}, f32[10,128,128]{2,1,0:T(8,128)S(1)}, u32[]{:S(2)}, u32[]{:S(2)}) %collective-permute-start.2) | collective-permute-done | bytes 655392 | tf_op jit(solution)/shard_map/ppermute | solution.py:362
  55.2 0.0 collective-permute-start.3
  55.2 0.0 collective-permute-done.1.info.info_b
  55.2 0.0 copy-start
  55.2 1.2 copy-done
  56.4 13.4 %shard_map.60 = (f32[512,512]{1,0:T(8,128)S(1)}, f32[4,128,128]{2,1,0:T(8,128)S(1)}, f32[512,512]{1,0:T(8,128)S(1)}) custom-call(f32[10,128,128]{2,1,0:T(8,128)S(1)} %get-tuple-element.25.mine, f32[10,128,128]{2,1,0:T(8,128)S(1)} %collective-permute-done.2.other, f32[512,512]{1,0:T(8,128)S(1)} %copy-done), custom_call_target="tpu_custom_call" | custom-call | flops 1000 | bytes 1000 | tf_op jit(solution)/shard_map/pallas_call | solution.py:29
  69.8 1.6 collective-permute-start.6
  71.4 0.0 collective-permute-done.4.rr_low
  71.4 8.4 %collective-permute-done.3.rs_other = f32[256,512]{1,0:T(8,128)S(1)} collective-permute-done((f32[256,512]{1,0:T(8,128)S(1)}, f32[256,512]{1,0:T(8,128)S(1)}, u32[]{:S(2)}, u32[]{:S(2)}) %collective-permute-start.3) | collective-permute-done | bytes 524320 | tf_op jit(solution)/shard_map/ppermute | solution.py:362
  79.8 0.0 collective-permute-start.5
  79.8 1.2 shard_map.61.v_first
  81.0 23.6 %collective-permute-done.5.rs_other = f32[256,512]{1,0:T(8,128)S(1)} collective-permute-done((f32[256,512]{1,0:T(8,128)S(1)}, f32[256,512]{1,0:T(8,128)S(1)}, u32[]{:S(2)}, u32[]{:S(2)}) %collective-permute-start.5) | collective-permute-done | bytes 524320 | tf_op jit(solution)/shard_map/ppermute | solution.py:362
  104.6 0.0 collective-permute-done.6.v_mine
  104.6 0.0 collective-permute-start.9
  104.7 1.5 collective-permute-start.7
  106.2 1.2 shard_map.62.v_second
  107.4 0.5 collective-permute-start.8
  107.9 5.7 %shard_map.63 = (f32[1536,512]{1,0:T(8,128)}, f32[1024,1024]{1,0:T(8,128)S(1)}) custom-call(f32[512,512]{1,0:T(8,128)S(1)} %get-tuple-element.28.lower, f32[512,512]{1,0:T(8,128)S(1)} %get-tuple-element.29.v_mine, f32[256,512]{1,0:T(8,128)S(1)} %shard_map.61.v_first, f32[256,512]{1,0:T(8,128)S(1)} %shard_map.62.v_second, ...), custom_call_target="tpu_custom_call" | custom-call | flops 1000 | bytes 1000 | tf_op jit(solution)/shard_map/pallas_call | solution.py:29
  113.7 5.8 %collective-permute-done.7.v_first = f32[256,512]{1,0:T(8,128)S(1)} collective-permute-done((f32[256,512]{1,0:T(8,128)S(1)}, f32[256,512]{1,0:T(8,128)S(1)}, u32[]{:S(2)}, u32[]{:S(2)}) %collective-permute-start.7) | collective-permute-done | bytes 524320 | tf_op jit(solution)/shard_map/ppermute | solution.py:362
  119.4 10.3 %collective-permute-done.8.v_second = f32[256,512]{1,0:T(8,128)S(1)} collective-permute-done((f32[256,512]{1,0:T(8,128)S(1)}, f32[256,512]{1,0:T(8,128)S(1)}, u32[]{:S(2)}, u32[]{:S(2)}) %collective-permute-start.8) | collective-permute-done | bytes 524320 | tf_op jit(solution)/shard_map/ppermute | solution.py:362
  129.7 6.2 %collective-permute-done.9.low_a = f32[10,128,128]{2,1,0:T(8,128)S(1)} collective-permute-done((f32[10,128,128]{2,1,0:T(8,128)S(1)}, f32[10,128,128]{2,1,0:T(8,128)S(1)}, u32[]{:S(2)}, u32[]{:S(2)}) %collective-permute-start.9) | collective-permute-done | bytes 655392 | tf_op jit(solution)/shard_map/ppermute | solution.py:362
  136.0 1.5 collective-permute-start.10
  137.4 3.9 %shard_map.64.up_b = f32[1024,1024]{1,0:T(8,128)S(1)} custom-call(f32[512,512]{1,0:T(8,128)S(1)} %collective-permute-done.6.v_mine, f32[256,512]{1,0:T(8,128)S(1)} %collective-permute-done.7.v_first, f32[256,512]{1,0:T(8,128)S(1)} %collective-permute-done.8.v_second, f32[10,128,128]{2,1,0:T(8,128)S(1)} %collective-permute-done.4.rr_low, ...), custom_call_target="tpu_custom_call" | custom-call | flops 1000 | bytes 1000 | tf_op jit(solution)/shard_map/pallas_call | solution.py:29
  141.3 11.3 %collective-permute-done.10.low_b = f32[10,128,128]{2,1,0:T(8,128)S(1)} collective-permute-done((f32[10,128,128]{2,1,0:T(8,128)S(1)}, f32[10,128,128]{2,1,0:T(8,128)S(1)}, u32[]{:S(2)}, u32[]{:S(2)}) %collective-permute-start.10) | collective-permute-done | bytes 655392 | tf_op jit(solution)/shard_map/ppermute | solution.py:362
  152.6 27.4 %shard_map.65 = (f32[1536,512]{1,0:T(8,128)}, f32[1024,1024]{1,0:T(8,128)}) custom-call(f32[1024,1024]{1,0:T(8,128)S(1)} %get-tuple-element.37.up_a, f32[1024,1024]{1,0:T(8,128)S(1)} %shard_map.64.up_b, f32[10,128,128]{2,1,0:T(8,128)S(1)} %collective-permute-done.9.low_a, f32[10,128,128]{2,1,0:T(8,128)S(1)} %collective-permute-done.10.low_b, ...), custom_call_target="tpu_custom_call" | custom-call | flops 1000 | bytes 1000 | tf_op jit(solution)/shard_map/pallas_call | solution.py:29
  (1 shorter events, 0.0 us)
Async XLA Ops:
  0.6 23.4 %collective-permute-start = (s32[1,8]{1,0:T(1,128)}, s32[1,8]{1,0:T(1,128)S(1)}, u32[]{:S(2)}, u32[]{:S(2)}) collective-permute-start(s32[1,8]{1,0:T(1,128)} %place.3), channel_id=1, source_target_pairs={{0,16},{8,24},{16,0},{24,8},{1,17},{9,25},{17,1},{25,9},{2,18},{10... | collective-permute-start | bytes 104 | tf_op jit(solution)/shard_map/ppermute | solution.py:362
  4.7 0.7 copy-start.1
  24.0 31.2 %collective-permute-start.2 = (f32[10,128,128]{2,1,0:T(8,128)S(1)}, f32[10,128,128]{2,1,0:T(8,128)S(1)}, u32[]{:S(2)}, u32[]{:S(2)}) collective-permute-start(f32[10,128,128]{2,1,0:T(8,128)S(1)} %get-tuple-element.25.mine), channel_id=1, source_target_pairs={{0,16},{8,24},{16,0},{24,8},{1,17},{9,25},{17,1},{25,9},{2,18},{10... | collective-permute-start | bytes 1966088 | tf_op jit(solution)/shard_map/ppermute | solution.py:362
  24.1 6.8 %copy-start.2 = (s32[1,8]{1,0:T(1,128)S(1)}, s32[1,8]{1,0:T(1,128)}, u32[]{:S(2)}) copy-start(s32[1,8]{1,0:T(1,128)} %param.5) | copy-start | bytes 100
  29.0 42.4 %collective-permute-start.4 = (f32[10,128,128]{2,1,0:T(8,128)S(1)}, f32[10,128,128]{2,1,0:T(8,128)S(1)}, u32[]{:S(2)}, u32[]{:S(2)}) collective-permute-start(f32[10,128,128]{2,1,0:T(8,128)S(1)} %get-tuple-element.39.rr_low), channel_id=1, source_target_pairs={{0,4},{1,5},{2,6},{3,7},{4,0},{5,1},{6,2},{7,3},{8,12},{9,13},{10,... | collective-permute-start | bytes 1966088 | tf_op jit(solution)/shard_map/ppermute | solution.py:362
  30.9 24.3 %collective-permute-start.1 = (s32[3,8]{1,0:T(4,128)S(1)}, s32[3,8]{1,0:T(4,128)S(1)}, u32[]{:S(2)}, u32[]{:S(2)}) collective-permute-start(s32[3,8]{1,0:T(4,128)S(1)} %pad_add_fusion.info.info_a), channel_id=1, source_target_pairs={{0,4},{1,5},{2,6},{3,7},{4,0},{5,1},{6,2},{7,3},{8,12},{9,13},{10,... | collective-permute-start | bytes 296 | tf_op jit(solution)/shard_map/ppermute | solution.py:362
  55.2 24.6 %collective-permute-start.3 = (f32[256,512]{1,0:T(8,128)S(1)}, f32[256,512]{1,0:T(8,128)S(1)}, u32[]{:S(2)}, u32[]{:S(2)}) collective-permute-start(f32[256,512]{1,0:T(8,128)S(1)} %get-tuple-element.32), channel_id=1, source_target_pairs={{0,16},{8,24},{16,0},{24,8},{1,17},{9,25},{17,1},{25,9},{2,18},{10... | collective-permute-start | bytes 1572872 | tf_op jit(solution)/shard_map/ppermute | solution.py:362
  55.2 1.2 copy-start
  69.8 34.8 %collective-permute-start.6 = (f32[512,512]{1,0:T(8,128)S(1)}, f32[512,512]{1,0:T(8,128)S(1)}, u32[]{:S(2)}, u32[]{:S(2)}) collective-permute-start(f32[512,512]{1,0:T(8,128)S(1)} %get-tuple-element.29.v_mine), channel_id=1, source_target_pairs={{0,4},{1,5},{2,6},{3,7},{4,0},{5,1},{6,2},{7,3},{8,12},{9,13},{10,... | collective-permute-start | bytes 3145736 | tf_op jit(solution)/shard_map/ppermute | solution.py:362
  79.8 24.8 %collective-permute-start.5 = (f32[256,512]{1,0:T(8,128)S(1)}, f32[256,512]{1,0:T(8,128)S(1)}, u32[]{:S(2)}, u32[]{:S(2)}) collective-permute-start(f32[256,512]{1,0:T(8,128)S(1)} %get-tuple-element.35), channel_id=1, source_target_pairs={{0,16},{8,24},{16,0},{24,8},{1,17},{9,25},{17,1},{25,9},{2,18},{10... | collective-permute-start | bytes 1572872 | tf_op jit(solution)/shard_map/ppermute | solution.py:362
  104.6 31.3 %collective-permute-start.9 = (f32[10,128,128]{2,1,0:T(8,128)S(1)}, f32[10,128,128]{2,1,0:T(8,128)S(1)}, u32[]{:S(2)}, u32[]{:S(2)}) collective-permute-start(f32[10,128,128]{2,1,0:T(8,128)S(1)} %get-tuple-element.39.rr_low), channel_id=1, source_target_pairs={{0,16},{8,24},{16,0},{24,8},{1,17},{9,25},{17,1},{25,9},{2,18},{10... | collective-permute-start | bytes 1966088 | tf_op jit(solution)/shard_map/ppermute | solution.py:362
  104.7 14.8 %collective-permute-start.7 = (f32[256,512]{1,0:T(8,128)S(1)}, f32[256,512]{1,0:T(8,128)S(1)}, u32[]{:S(2)}, u32[]{:S(2)}) collective-permute-start(f32[256,512]{1,0:T(8,128)S(1)} %shard_map.61.v_first), channel_id=1, source_target_pairs={{0,4},{1,5},{2,6},{3,7},{4,0},{5,1},{6,2},{7,3},{8,12},{9,13},{10,... | collective-permute-start | bytes 1572872 | tf_op jit(solution)/shard_map/ppermute | solution.py:362
  107.4 22.3 %collective-permute-start.8 = (f32[256,512]{1,0:T(8,128)S(1)}, f32[256,512]{1,0:T(8,128)S(1)}, u32[]{:S(2)}, u32[]{:S(2)}) collective-permute-start(f32[256,512]{1,0:T(8,128)S(1)} %shard_map.62.v_second), channel_id=1, source_target_pairs={{0,4},{1,5},{2,6},{3,7},{4,0},{5,1},{6,2},{7,3},{8,12},{9,13},{10,... | collective-permute-start | bytes 1572872 | tf_op jit(solution)/shard_map/ppermute | solution.py:362
  136.0 16.7 %collective-permute-start.10 = (f32[10,128,128]{2,1,0:T(8,128)S(1)}, f32[10,128,128]{2,1,0:T(8,128)S(1)}, u32[]{:S(2)}, u32[]{:S(2)}) collective-permute-start(f32[10,128,128]{2,1,0:T(8,128)S(1)} %collective-permute-done.9.low_a), channel_id=1, source_target_pairs={{0,4},{1,5},{2,6},{3,7},{4,0},{5,1},{6,2},{7,3},{8,12},{9,13},{10,... | collective-permute-start | bytes 1966088 | tf_op jit(solution)/shard_map/ppermute | solution.py:362

commit v2 on v1

v2 whole, which is shorter than its diff:
```python
import jax
import jax.numpy as jnp
from jax import lax
from jax.experimental import pallas as pl
from jax.experimental.pallas import tpu as pltpu
from jax.sharding import PartitionSpec as P

f32 = jnp.float32
bf16 = jnp.bfloat16
NT = (((1,), (1,)), ((), ()))
TN = (((0,), (0,)), ((), ()))
BLK = 128
KB = 8
KS = 4
NS = KS * BLK
NB = KB * BLK
NJ = NS + NB
BELOW = [(a, b) for a in range(KS) for b in range(a)]
PACKED = len(BELOW) + KS // 2
FIRST = PACKED - 3
VMEM = pl.BlockSpec(memory_space=pltpu.VMEM)
SMEM = pl.BlockSpec(memory_space=pltpu.SMEM)
HBM = pl.BlockSpec(memory_space=pltpu.HBM)


def sds(*shape):
    return jax.ShapeDtypeStruct(shape, f32)


def call(body, out, ins, outs, scratch, args, vmem=24, us=0):
    return pl.pallas_call(
        body,
        out_shape=out,
        in_specs=ins,
        out_specs=outs,
        scratch_shapes=scratch,
        cost_estimate=pl.CostEstimate(flops=1000, bytes_accessed=1000 + int(us * 3.5e6), transcendentals=0),
        compiler_params=pltpu.CompilerParams(vmem_limit_bytes=vmem * 1024 * 1024),
    )(*args)


def split(x):
    hi = x.astype(bf16)
    return hi, (x - hi.astype(f32)).astype(bf16)


def dot(a, b, dims):
    return lax.dot_general(a, b, dims, preferred_element_type=f32)


def mm3(a, b):
    return dot(jnp.concatenate([a[0], a[0], a[1]], 1), jnp.concatenate([b[0], b[1], b[0]], 1), NT)


def row(x, k):
    return jnp.broadcast_to(x[k : k + 1, :], x.shape)


def col(x, j):
    return jnp.broadcast_to(x[:, j : j + 1], (8, BLK))


def pack(blocks, out):
    ri = lax.broadcasted_iota(jnp.int32, (BLK, BLK), 0)
    ci = lax.broadcasted_iota(jnp.int32, (BLK, BLK), 1)
    for n, key in enumerate(BELOW):
        out(n, blocks[key])
    diagonals = []
    for n in range(KS // 2):
        one, two = blocks[2 * n, 2 * n], blocks[2 * n + 1, 2 * n + 1]
        out(len(BELOW) + n, jnp.where(ri >= ci, one, two))
        diagonals.append(jnp.sum(jnp.where(ri == ci, two, 0.0), axis=0, keepdims=True))
    return jnp.concatenate(diagonals + [jnp.zeros((8 - len(diagonals), BLK), f32)], 0)


def unpack(packed, tail):
    ri = lax.broadcasted_iota(jnp.int32, (BLK, BLK), 0)
    ci = lax.broadcasted_iota(jnp.int32, (BLK, BLK), 1)
    blocks = {}
    for n, block in packed.items():
        turned = block.T
        if n < len(BELOW):
            i, j = BELOW[n]
            blocks[i, j], blocks[j, i] = block, turned
        else:
            m = 2 * (n - len(BELOW))
            diagonal = jnp.broadcast_to(tail[m // 2 : m // 2 + 1, :], (BLK, BLK))
            blocks[m, m] = jnp.where(ri >= ci, block, turned)
            blocks[m + 1, m + 1] = jnp.where(ri < ci, block, jnp.where(ri > ci, turned, diagonal))
    return blocks


def rows_of(ref, first=0):
    return {first + n: ref[BLK * n : BLK * n + BLK, :] for n in range(ref.shape[0] // BLK)}


def unpack_all(ref):
    return unpack(rows_of(ref), ref[BLK * PACKED :, :])


def unpack_first(ref):
    return unpack(rows_of(ref), None)


def unpack_second(ref):
    return unpack(rows_of(ref, FIRST), ref[BLK * (PACKED - FIRST) :, :])


def factor_block(block):
    ri = lax.broadcasted_iota(jnp.int32, (8, BLK), 0)
    ci = lax.broadcasted_iota(jnp.int32, (8, BLK), 1)
    count, wide = BLK // 8, 4
    left = [block[8 * t : 8 * t + 8, :] for t in range(count)]
    right = [jnp.where(ci == ri + 8 * t, 1.0, 0.0).astype(f32) for t in range(count)]
    upper, inverse = [], []
    here = [col(left[0], k) for k in range(8)]
    for s in range(count):
        end = (s // wide + 1) * wide
        ahead = {w: [col(left[w], 8 * s + k) for k in range(8)] for w in range(s + 1, min(end + 1, count))}
        following = [col(left[s + 1], 8 * s + 8 + k) for k in range(8)] if s + 1 < count else None
        a, t = left[s], right[s]
        pivots = None
        for k in range(8):
            pivot = row(here[k], k)
            inv = pl.reciprocal(pivot, approx=True)
            pivots = pivot if k == 0 else jnp.where(ri == k, pivot, pivots)
            mult = jnp.where(ri > k, here[k], 0.0) * inv
            rows = {m: row(here[m], k) for m in range(k + 1, 8)}
            row_a, row_t = row(a, k), row(t, k)
            for m in range(k + 1, 8):
                here[m] = here[m] - mult * rows[m]
            a = a - mult * row_a
            t = t - mult * row_t
            for w, cols in ahead.items():
                mult = cols[k] * inv
                if w == s + 1:
                    following = [f - mult * row(cols[k], m) for m, f in enumerate(following)]
                for m in range(k + 1, 8):
                    cols[m] = cols[m] - mult * rows[m]
                left[w] = left[w] - mult * row_a
                right[w] = right[w] - mult * row_t
        here = following
        scale = lax.rsqrt(pivots)
        upper.append(a * scale)
        inverse.append(t * scale)
        if s + 1 == end and end + 1 < count:
            ah, al = split(jnp.concatenate(upper[-wide:], 0))
            th, tl = split(jnp.concatenate(inverse[-wide:], 0))
            lhs = jnp.concatenate([ah, ah, al], 0)
            rhs_a = jnp.concatenate([ah, al, ah], 0)
            rhs_t = jnp.concatenate([th, tl, th], 0)
            outer = dot(lhs, jnp.concatenate([rhs_a, rhs_t], 1), TN)
            for q in range(end + 1, count):
                left[q] = left[q] - outer[8 * q : 8 * q + 8, :BLK]
                right[q] = right[q] - outer[8 * q : 8 * q + 8, BLK:]
    return jnp.concatenate(inverse, 0)


def factor(work, x, lower, inv, corner, ready=None):
    ri = lax.broadcasted_iota(jnp.int32, (NS, BLK), 0)
    ci = lax.broadcasted_iota(jnp.int32, (NS, BLK), 1)

    def finish(k, inverse):
        here = at(BLK * k)
        inv[k] = inverse
        lower[:, here] = jnp.where(ri >= ci + BLK * k, mm3(split(work[:, here]), split(inverse)), 0.0)
        if not isinstance(k, int) or k + 1 < KS:
            then = at(BLK * jnp.minimum(k + 1, KS - 1))
            pair = split(lower[then, here])
            corner[...] = work[then, then] - mm3(pair, pair)

    def update(k):
        here = at(BLK * k)
        pair = split(lower[:, here])
        work[...] = work[...] - mm3(pair, pair)
        done = mm3(split(x[:, here]), split(inv[k]))
        x[...] = x[...] - mm3(split(done), pair)
        x[:, here] = done

    def step(k, carry):
        inverse = factor_block(corner[...])
        update(k - 1)
        finish(k, inverse)
        return carry

    inverse = factor_block(work[0:BLK, 0:BLK])
    if ready is not None:
        ready()
    finish(0, inverse)
    lax.fori_loop(1, KS, step, 0)
    x[:, NS - BLK :] = mm3(split(x[:, NS - BLK :]), split(inv[KS - 1]))


def solve(x, lower, inv):
    for k in range(KS):
        o, e = BLK * k, BLK * (k + 1)
        done = mm3(split(x[:, o:e]), split(inv[k]))
        x[:, o:e] = done
        if k + 1 < KS:
            x[:, e:] = x[:, e:] - mm3(split(done), split(lower[e:, o:e]))


def ranks(values):
    out = []
    for a, va in enumerate(values):
        r = jnp.int32(0)
        for b, vb in enumerate(values):
            if a != b:
                r = r + (vb < va).astype(jnp.int32)
        out.append(r)
    return out


def sort_blocks(place, order):
    values = [place[0, a] for a in range(KB)]
    for a, r in enumerate(ranks(values)):
        order[r] = jnp.int32(a)


def at(start):
    return pl.ds(pl.multiple_of(start, BLK), BLK)


def corner_of(ref):
    return {
        (i, j): ref[BLK * i : BLK * i + BLK, BLK * j : BLK * j + BLK] for i in range(KS) for j in range(i + 1)
    }


def leaf_a(front, place, corner, w_out, a, lower, inv, next_block, ss, order, sems):
    sort_blocks(place, order)
    copies = []
    for rows in (slice(0, BLK), slice(BLK, NS)):
        c = pltpu.make_async_copy(front.at[rows, 0:NS], a.at[rows, :], sems.at[len(copies)])
        c.start()
        copies.append(c)
    for t in range(KB):
        c = pltpu.make_async_copy(
            front.at[at(NS + BLK * order[t]), 0:NS], w_out.at[BLK * t : BLK * t + BLK, :], sems.at[len(copies)]
        )
        c.start()
        copies.append(c)
    for i in range(KS):
        for j in range(i + 1):
            c = pltpu.make_async_copy(
                front.at[at(NS + BLK * order[i]), at(NS + BLK * order[j])],
                ss.at[BLK * i : BLK * i + BLK, BLK * j : BLK * j + BLK],
                sems.at[len(copies)],
            )
            c.start()
            copies.append(c)
    copies[0].wait()

    def ready():
        for c in copies[1:]:
            c.wait()

    factor(a, w_out, lower, inv, next_block, ready)
    w = split(w_out[0:NS, :])
    gram = mm3(w, w)
    blocks = {}
    for i in range(KS):
        for j in range(i + 1):
            rows, cols = slice(BLK * i, BLK * i + BLK), slice(BLK * j, BLK * j + BLK)
            blocks[i, j] = ss[rows, cols] - gram[rows, cols]

    def out(n, block):
        corner[BLK * n : BLK * n + BLK, :] = block

    corner[BLK * PACKED :, :] = pack(blocks, out)


def leaf_b(front, place, w, rs, rr_all, rr_a, rr_b, f_rs, f_rr, order, sems):
    sort_blocks(place, order)
    copies = []
    for i in range(KS):
        for j in range(KB):
            dst = f_rs if j < KS else f_rr
            c = pltpu.make_async_copy(
                front.at[at(NS + BLK * order[KS + i]), at(NS + BLK * order[j])],
                dst.at[BLK * i : BLK * i + BLK, BLK * (j % KS) : BLK * (j % KS) + BLK],
                sems.at[i * KB + j],
            )
            c.start()
            copies.append(c)
    ws, wr = split(w[0:NS, :]), split(w[NS:, :])
    g_rs = mm3(wr, ws)
    g_rr = mm3(wr, wr)
    for c in copies:
        c.wait()
    rs[...] = f_rs[...] - g_rs
    f_rr[...] = f_rr[...] - g_rr

    def out(n, block):
        rr_all[BLK * n : BLK * n + BLK, :] = block
        if n < FIRST:
            rr_a[BLK * n : BLK * n + BLK, :] = block
        else:
            rr_b[BLK * (n - FIRST) : BLK * (n - FIRST) + BLK, :] = block

    tail = pack(corner_of(f_rr), out)
    rr_all[BLK * PACKED :, :] = tail
    rr_b[BLK * (PACKED - FIRST) :, :] = tail


def merge_a(mine, other, rs, lower, inv, v, work, next_block):
    packed = {n: block + other[BLK * n : BLK * n + BLK, :] for n, block in rows_of(mine).items()}
    tail = mine[BLK * PACKED :, :] + other[BLK * PACKED :, :]
    for (i, j), block in unpack(packed, tail).items():
        work[BLK * i : BLK * i + BLK, BLK * j : BLK * j + BLK] = block
    v[...] = rs[...]
    factor(work, v, lower, inv, next_block)


def canonical(info, order):
    places = []
    for r in range(2):
        row_of = info.at[r : r + 1]
        sort_blocks(row_of, order)
        places += [row_of[0, order[KS + i]] for i in range(KS)]
    return [info[2, p - KS] for p in places]


def row_blocks(*parts):
    return [v.at[o : o + BLK, :] for v in parts for o in range(0, v.shape[0], BLK)]


def pair_update(rows, rr_low, spots, update, vs):
    where = ranks(spots)
    for e in range(KB):
        vs[at(BLK * where[e]), :] = rows[e][...]
    top, low = split(vs[0:NS, :]), split(vs[NS:, :])
    update[0:NS, 0:NS] = -mm3(top, top)
    update[NS:, 0:NS] = -mm3(low, top)
    update[NS:, NS:] = -mm3(low, low)
    for (i, j), block in unpack_all(rr_low).items():
        r, c = at(BLK * where[i]), at(BLK * where[j])
        update[r, c] = update[r, c] + block


def merge_b(lower, inv, rs_other, v):
    v[...] = rs_other[...]
    solve(v, lower, inv)


def assemble_mine(lower, v_mine, v_other, rr_low, info, panel, update, vs, order):
    rows = row_blocks(v_mine, v_other)
    pair_update(rows, rr_low, canonical(info, order), update, vs)
    panel[0:NS, :] = lower[...]
    for r in range(2):
        row_of = info.at[r : r + 1]
        sort_blocks(row_of, order)
        for i in range(KS):
            panel[at(BLK * row_of[0, order[KS + i]]), :] = rows[KS * r + i][...]


def assemble_other(v_mine, v_other, rr_low, info, update, vs, order):
    pair_update(row_blocks(v_mine, v_other), rr_low, canonical(info, order), update, vs)


def add_blocks(blocks, spots, ss, x, rr):
    for (i, j), block in blocks.items():
        si, sj = spots[i], spots[j]

        @pl.when((si < KS) & (sj < KS))
        def _():
            r, c = at(BLK * si), at(BLK * sj)
            ss[r, c] = ss[r, c] + block

        @pl.when((si >= KS) & (sj < KS))
        def _():
            r, c = at(BLK * (si - KS)), at(BLK * sj)
            x[r, c] = x[r, c] + block

        @pl.when((si >= KS) & (sj >= KS))
        def _():
            r, c = at(BLK * (si - KS)), at(BLK * (sj - KS))
            rr[r, c] = rr[r, c] + block


def join(up_a, up_b, low_a1, low_a2, low_b1, info_a, info_b, ss, x, rr, order):
    ss[...] = up_a[0:NS, 0:NS] + up_b[0:NS, 0:NS]
    rr[...] = jnp.zeros((NB, NB), f32)
    far = []
    for up, info in ((up_a, info_a), (up_b, info_b)):
        spots = canonical(info, order)
        far.append(spots[KS:])
        for spot, rank in zip(spots, ranks(spots)):
            order[rank] = spot
        for i in range(KS):
            r = at(BLK * (order[KS + i] - KS))
            rows = slice(NS + BLK * i, NS + BLK * i + BLK)
            x[r, :] = up[rows, 0:NS]
            for j in range(KS):
                rr[r, at(BLK * (order[KS + j] - KS))] = up[rows, NS + BLK * j : NS + BLK * j + BLK]
    add_blocks(unpack_first(low_a1), far[0], ss, x, rr)
    add_blocks(unpack_second(low_a2), far[0], ss, x, rr)
    add_blocks(unpack_first(low_b1), far[1], ss, x, rr)


def last(ss, x_in, rr, low, info, panel, update, work, x, lower, inv, next_block, buf, order, sems):
    fill = pltpu.make_async_copy(rr, buf, sems.at[0])
    fill.start()
    work[...] = ss[...]
    x[...] = x_in[...]
    far = canonical(info, order)[KS:]
    blocks = unpack_second(low)
    fill.wait()
    add_blocks(blocks, far, work, x, buf)
    factor(work, x, lower, inv, next_block)
    outs = [
        pltpu.make_async_copy(lower, panel.at[0:NS, :], sems.at[1]),
        pltpu.make_async_copy(x, panel.at[NS:, :], sems.at[2]),
    ]
    for c in outs:
        c.start()
    pair = split(x[...])
    wide = 2 * BLK
    for t in range(NB // wide):
        cols = slice(wide * t, wide * t + wide)
        buf[:, cols] = buf[:, cols] - mm3(pair, tuple(p[cols] for p in pair))
        c = pltpu.make_async_copy(buf.at[:, cols], update.at[:, cols], sems.at[3 + t])
        c.start()
        outs.append(c)
    for c in outs:
        c.wait()


def after(x, *earlier):
    return lax.optimization_barrier((x,) + earlier)[0]


def shards(leaf_front, place_pairs, place_quads):
    dma = pltpu.SemaphoreType.DMA
    half_cols = lax.axis_size("gx") // 2
    half_rows = lax.axis_size("gy") // 2

    def partner(x, axis):
        half = half_cols if axis == "gx" else half_rows
        return lax.ppermute(x, axis, [(i, (i + half) % (2 * half)) for i in range(2 * half)])

    def vmem(*shape):
        return pltpu.VMEM(shape, f32)

    order = pltpu.SMEM((KB,), jnp.int32)
    factor_scratch = [vmem(NS, NS), vmem(KS, BLK, BLK), vmem(BLK, BLK)]
    tri = sds(BLK * PACKED + 8, BLK)
    tri_a, tri_b = sds(BLK * FIRST, BLK), sds(BLK * (PACKED - FIRST) + 8, BLK)

    pairs_other = partner(place_pairs, "gx")
    corner, w = call(
        leaf_a, (tri, sds(NB, NS)), [HBM, SMEM], [VMEM, VMEM],
        [vmem(NS, NS)] + factor_scratch + [vmem(NS, NS), order, dma((2 + KB + KS * (KS + 1) // 2,))],
        (leaf_front, place_pairs), 48)
    corner_other = partner(after(corner, pairs_other), "gx")
    rs, rr, rr_a, rr_b = call(
        leaf_b, (sds(NS, NS), tri, tri_a, tri_b), [HBM, SMEM, VMEM], [VMEM] * 4,
        [vmem(NS, NS), vmem(NS, NS), order, dma((KS * KB,))], (leaf_front, place_pairs, w), 48)
    rr_far = partner(rr, "gy")
    info = jnp.concatenate([place_pairs, pairs_other, place_quads], 0)
    info_other = partner(info, "gy")
    corner, info_other = lax.optimization_barrier((corner, info_other))
    rs_other = partner(after(rs, corner_other), "gx")

    lower, inv, v_mine = call(
        merge_a, (sds(NS, NS), sds(KS, BLK, BLK), sds(NS, NS)), [VMEM] * 3, [VMEM] * 3,
        [vmem(NS, NS), vmem(BLK, BLK)], (corner, corner_other, rs), us=13)
    v_mine_far = partner(after(v_mine, rr_far), "gy")
    rr_first = partner(after(rr_a, v_mine_far), "gx")
    v_other = call(merge_b, sds(NS, NS), [VMEM] * 3, VMEM, [], (lower, inv, rs_other))
    v_other_far = partner(v_other, "gy")
    scratch = [vmem(NB, NS), order]
    pair_panel, update = call(
        assemble_mine, (sds(NS + NB, NS), sds(NB, NB)), [VMEM] * 4 + [SMEM], [VMEM] * 2, scratch,
        (lower, v_mine, v_other, rr, info))
    rr_first, update = lax.optimization_barrier((rr_first, update))
    rr_second = partner(after(rr_b, rr_first), "gx")
    rr_first_far = partner(rr_first, "gy")
    update_far = call(
        assemble_other, sds(NB, NB), [VMEM] * 3 + [SMEM], VMEM, scratch,
        (v_mine_far, v_other_far, rr_far, info_other))
    rr_second_far = partner(after(rr_second, update_far, rr_first_far), "gy")
    ss, x, rr = call(
        join, (sds(NS, NS), sds(NB, NS), sds(NB, NB)), [VMEM] * 5 + [SMEM] * 2, [VMEM] * 3, [order],
        (update, update_far, rr_first, rr_second, rr_first_far, info, info_other))
    quad_panel, quad_update = call(
        last, (sds(NS + NB, NS), sds(NB, NB)), [VMEM] * 4 + [SMEM], [HBM, HBM],
        [vmem(NS, NS), vmem(NB, NS)] + factor_scratch + [vmem(NB, NB), order, dma((3 + KB,))],
        (ss, x, rr, rr_second_far, info_other))
    return pair_panel, quad_panel, quad_update


def solution(mesh):
    spec = P("gx", "gy")
    return jax.shard_map(
        shards, mesh=mesh, in_specs=(spec, spec, spec), out_specs=(spec, spec, spec), check_vma=False
    )
```

time: 180 us -> 156 us (0.87)
  waiting for transfers between devices: 89.7 us -> 72.7 us
  Pallas kernels: 76.1 us -> 68.5 us
    ppermute x11, waiting for transfers between devices: 89.7 us -> 72.7 us  [partner(): lax.ppermute(x, axis, [(i, (i + half) % (2 * half)) for i in range(2 * ha...]
    pallas_call x8, Pallas kernels: 76.1 us -> 68.5 us  [call(): pl.pallas_call(body, out_shape=out, in_specs=ins, out_specs=outs, scratch...]
  transfers between devices with their start and end apart: 11 -> 11, of which waited for: 7 -> 7; matrix products, arithmetic and copies ran while one was open for 0% -> 0% of each run, Pallas kernels for 27% -> 31%
where the time goes in v2:
time: 156 us
  waiting for transfers between devices  72.7 us (47%)
  Pallas kernels  68.5 us (44%)
  starting transfers between devices  12.9 us (8%)
    ppermute x11, waiting for transfers between devices, partner(): lax.ppermute(x, axis, [(i, (i + half) % (2 * half)) for i in range(2 * ha...  72.7 us
    pallas_call x8, Pallas kernels, call(): pl.pallas_call(body, out_shape=out, in_specs=ins, out_specs=outs, scratch...  68.5 us
    ppermute x11, starting transfers between devices, partner(): lax.ppermute(x, axis, [(i, (i + half) % (2 * half)) for i in range(2 * ha...  12.9 us
  transfers between devices with their start and end apart: 11, of which 7 were waited for; matrix products, arithmetic and copies ran while one was open for 0% of the time, Pallas kernels for 31%

profile of v2, /device:TPU:0, one launch (start us, length us, event | category | flops | bytes accessed | tf_op | source)
XLA Modules:
  0.0 155.8 jit_solution(10054077182335857253)
XLA Ops:
  0.6 4.1 %collective-permute-start = (s32[1,8]{1,0:T(1,128)}, s32[1,8]{1,0:T(1,128)S(1)}, u32[]{:S(2)}, u32[]{:S(2)}) collective-permute-start(s32[1,8]{1,0:T(1,128)} %place.3), channel_id=1, source_target_pairs={{0,16},{8,24},{16,0},{24,8},{1,17},{9,25},{17,1},{25,9},{2,18},{10... | collective-permute-start | bytes 104 | tf_op jit(solution)/shard_map/ppermute | solution.py:440
  4.7 0.0 copy-start
  4.7 0.7 copy-done
  5.4 17.0 %shard_map.58 = (f32[1032,128]{1,0:T(8,128)S(1)}, f32[1024,512]{1,0:T(8,128)S(1)}) custom-call(f32[1536,1536]{1,0:T(8,128)} %front.3, s32[1,8]{1,0:T(1,128)S(1)} %copy-done), custom_call_target="tpu_custom_call" | custom-call | flops 1000 | bytes 1000 | tf_op jit(solution)/shard_map/pallas_call | solution.py:31
  22.4 0.0 collective-permute-done
  22.4 0.1 collective-permute-start.2
  22.5 0.0 copy-start.1
  22.5 3.7 %shard_map.59 = (f32[512,512]{1,0:T(8,128)S(1)}, f32[1032,128]{1,0:T(8,128)S(1)}, f32[640,128]{1,0:T(8,128)S(1)}, f32[392,128]{1,0:T(8,128)S(1)}) custom-call(f32[1536,1536]{1,0:T(8,128)} %front.3, s32[1,8]{1,0:T(1,128)S(1)} %copy-done, f32[1024,512]{1,0:T(8,128)S(1)} %get-tuple-element.32.w), custom_call_target="tpu_custom_call" | custom-call | flops 1000 | bytes 1000 | tf_op jit(solution)/shard_map/pallas_call | solution.py:31
  26.2 1.9 %collective-permute-start.4 = (f32[1032,128]{1,0:T(8,128)S(1)}, f32[1032,128]{1,0:T(8,128)S(1)}, u32[]{:S(2)}, u32[]{:S(2)}) collective-permute-start(f32[1032,128]{1,0:T(8,128)S(1)} %get-tuple-element.38.rr_low), channel_id=1, source_target_pairs={{0,4},{1,5},{2,6},{3,7},{4,0},{5,1},{6,2},{7,3},{8,12},{9,13},{10,... | collective-permute-start | bytes 1585160 | tf_op jit(solution)/shard_map/ppermute | solution.py:440
  28.1 20.1 %collective-permute-done.2.other = f32[1032,128]{1,0:T(8,128)S(1)} collective-permute-done((f32[1032,128]{1,0:T(8,128)S(1)}, f32[1032,128]{1,0:T(8,128)S(1)}, u32[]{:S(2)}, u32[]{:S(2)}) %collective-permute-start.2) | collective-permute-done | bytes 528416 | tf_op jit(solution)/shard_map/ppermute | solution.py:440
  48.2 0.0 collective-permute-start.3
  48.2 0.0 copy-done.1
  48.2 1.6 %collective-permute-start.1 = (s32[3,8]{1,0:T(4,128)S(1)}, s32[3,8]{1,0:T(4,128)S(1)}, u32[]{:S(2)}, u32[]{:S(2)}) collective-permute-start(s32[3,8]{1,0:T(4,128)S(1)} %pad_add_fusion.info.info_a), channel_id=1, source_target_pairs={{0,4},{1,5},{2,6},{3,7},{4,0},{5,1},{6,2},{7,3},{8,12},{9,13},{10,... | collective-permute-start | bytes 296 | tf_op jit(solution)/shard_map/ppermute | solution.py:440
  49.8 2.1 %collective-permute-done.1.info.info_b = s32[3,8]{1,0:T(4,128)S(1)} collective-permute-done((s32[3,8]{1,0:T(4,128)S(1)}, s32[3,8]{1,0:T(4,128)S(1)}, u32[]{:S(2)}, u32[]{:S(2)}) %collective-permute-start.1) | collective-permute-done | bytes 128 | tf_op jit(solution)/shard_map/ppermute | solution.py:440
  51.8 13.4 %shard_map.60 = (f32[512,512]{1,0:T(8,128)S(1)}, f32[4,128,128]{2,1,0:T(8,128)S(1)}, f32[512,512]{1,0:T(8,128)S(1)}) custom-call(f32[1032,128]{1,0:T(8,128)S(1)} %get-tuple-element.31.mine, f32[1032,128]{1,0:T(8,128)S(1)} %collective-permute-done.2.other, f32[512,512]{1,0:T(8,128)S(1)} %get-tuple-element.37.rs), custom_call_target="tpu_custom_call" | custom-call | flops 1000 | bytes 45501000 | tf_op jit(solution)/shard_map/pallas_call | solution.py:31
  65.2 0.0 collective-permute-done.4.rr_low
  65.3 1.6 %collective-permute-start.5 = (f32[512,512]{1,0:T(8,128)S(1)}, f32[512,512]{1,0:T(8,128)S(1)}, u32[]{:S(2)}, u32[]{:S(2)}) collective-permute-start(f32[512,512]{1,0:T(8,128)S(1)} %get-tuple-element.41.v_mine), channel_id=1, source_target_pairs={{0,4},{1,5},{2,6},{3,7},{4,0},{5,1},{6,2},{7,3},{8,12},{9,13},{10,... | collective-permute-start | bytes 3145736 | tf_op jit(solution)/shard_map/ppermute | solution.py:440
  66.8 28.3 %collective-permute-done.3.rs_other = f32[512,512]{1,0:T(8,128)S(1)} collective-permute-done((f32[512,512]{1,0:T(8,128)S(1)}, f32[512,512]{1,0:T(8,128)S(1)}, u32[]{:S(2)}, u32[]{:S(2)}) %collective-permute-start.3) | collective-permute-done | bytes 1048608 | tf_op jit(solution)/shard_map/ppermute | solution.py:440
  95.2 1.5 shard_map.61.v_other
  96.7 1.6 %collective-permute-start.7 = (f32[512,512]{1,0:T(8,128)S(1)}, f32[512,512]{1,0:T(8,128)S(1)}, u32[]{:S(2)}, u32[]{:S(2)}) collective-permute-start(f32[512,512]{1,0:T(8,128)S(1)} %shard_map.61.v_other), channel_id=1, source_target_pairs={{0,4},{1,5},{2,6},{3,7},{4,0},{5,1},{6,2},{7,3},{8,12},{9,13},{10,... | collective-permute-start | bytes 3145736 | tf_op jit(solution)/shard_map/ppermute | solution.py:440
  98.3 0.0 collective-permute-done.5.v_mine
  98.3 0.0 collective-permute-start.6
  98.3 5.7 %shard_map.62 = (f32[1536,512]{1,0:T(8,128)}, f32[1024,1024]{1,0:T(8,128)S(1)}) custom-call(f32[512,512]{1,0:T(8,128)S(1)} %get-tuple-element.34.lower, f32[512,512]{1,0:T(8,128)S(1)} %get-tuple-element.41.v_mine, f32[512,512]{1,0:T(8,128)S(1)} %shard_map.61.v_other, f32[1032,128]{1,0:T(8,128)S(1)} %get-tuple-element.38.rr_low, ...), custom_call_target="tpu_custom_call" | custom-call | flops 1000 | bytes 1000 | tf_op jit(solution)/shard_map/pallas_call | solution.py:31
  104.0 10.4 %collective-permute-done.6.low_a1 = f32[640,128]{1,0:T(8,128)S(1)} collective-permute-done((f32[640,128]{1,0:T(8,128)S(1)}, f32[640,128]{1,0:T(8,128)S(1)}, u32[]{:S(2)}, u32[]{:S(2)}) %collective-permute-start.6) | collective-permute-done | bytes 327712 | tf_op jit(solution)/shard_map/ppermute | solution.py:440
  114.5 0.5 collective-permute-start.9
  115.0 0.0 collective-permute-start.8
  115.0 7.8 %collective-permute-done.7.v_other = f32[512,512]{1,0:T(8,128)S(1)} collective-permute-done((f32[512,512]{1,0:T(8,128)S(1)}, f32[512,512]{1,0:T(8,128)S(1)}, u32[]{:S(2)}, u32[]{:S(2)}) %collective-permute-start.7) | collective-permute-done | bytes 1048608 | tf_op jit(solution)/shard_map/ppermute | solution.py:440
  122.7 3.9 %shard_map.63.up_b = f32[1024,1024]{1,0:T(8,128)S(1)} custom-call(f32[512,512]{1,0:T(8,128)S(1)} %collective-permute-done.5.v_mine, f32[512,512]{1,0:T(8,128)S(1)} %collective-permute-done.7.v_other, f32[1032,128]{1,0:T(8,128)S(1)} %collective-permute-done.4.rr_low, s32[3,8]{1,0:T(4,128)S(1)} %collective-permute-done.1.info.info_b), custom_call_target="tpu_custom_call" | custom-call | flops 1000 | bytes 1000 | tf_op jit(solution)/shard_map/pallas_call | solution.py:31
  126.6 0.0 collective-permute-done.8.low_a2
  126.6 2.2 %collective-permute-done.9.low_b1 = f32[640,128]{1,0:T(8,128)S(1)} collective-permute-done((f32[640,128]{1,0:T(8,128)S(1)}, f32[640,128]{1,0:T(8,128)S(1)}, u32[]{:S(2)}, u32[]{:S(2)}) %collective-permute-start.9) | collective-permute-done | bytes 327712 | tf_op jit(solution)/shard_map/ppermute | solution.py:440
  128.8 1.6 %collective-permute-start.10 = (f32[392,128]{1,0:T(8,128)S(1)}, f32[392,128]{1,0:T(8,128)S(1)}, u32[]{:S(2)}, u32[]{:S(2)}) collective-permute-start(f32[392,128]{1,0:T(8,128)S(1)} %collective-permute-done.8.low_a2), channel_id=1, source_target_pairs={{0,4},{1,5},{2,6},{3,7},{4,0},{5,1},{6,2},{7,3},{8,12},{9,13},{10,... | collective-permute-start | bytes 602120 | tf_op jit(solution)/shard_map/ppermute | solution.py:440
  130.4 2.7 %shard_map.64 = (f32[512,512]{1,0:T(8,128)S(1)}, f32[1024,512]{1,0:T(8,128)S(1)}, f32[1024,1024]{1,0:T(8,128)S(1)}) custom-call(f32[1024,1024]{1,0:T(8,128)S(1)} %get-tuple-element.44.up_a, f32[1024,1024]{1,0:T(8,128)S(1)} %shard_map.63.up_b, f32[640,128]{1,0:T(8,128)S(1)} %collective-permute-done.6.low_a1, f32[392,128]{1,0:T(8,128)S(1)} %collective-permute-done.8.low_a2, ...), custom_call_target="tpu_custom_call" | custom-call | flops 1000 | bytes 1000 | tf_op jit(solution)/shard_map/pallas_call | solution.py:31
  133.1 1.8 %collective-permute-done.10.low = f32[392,128]{1,0:T(8,128)S(1)} collective-permute-done((f32[392,128]{1,0:T(8,128)S(1)}, f32[392,128]{1,0:T(8,128)S(1)}, u32[]{:S(2)}, u32[]{:S(2)}) %collective-permute-start.10) | collective-permute-done | bytes 200736 | tf_op jit(solution)/shard_map/ppermute | solution.py:440
  134.9 20.7 %shard_map.65 = (f32[1536,512]{1,0:T(8,128)}, f32[1024,1024]{1,0:T(8,128)}) custom-call(f32[512,512]{1,0:T(8,128)S(1)} %get-tuple-element.49.ss, f32[1024,512]{1,0:T(8,128)S(1)} %get-tuple-element.50.x_in, f32[1024,1024]{1,0:T(8,128)S(1)} %get-tuple-element.51.rr, f32[392,128]{1,0:T(8,128)S(1)} %collective-permute-done.10.low, ...), custom_call_target="tpu_custom_call" | custom-call | flops 1000 | bytes 1000 | tf_op jit(solution)/shard_map/pallas_call | solution.py:31
  (1 shorter events, 0.0 us)
Async XLA Ops:
  0.6 21.8 %collective-permute-start = (s32[1,8]{1,0:T(1,128)}, s32[1,8]{1,0:T(1,128)S(1)}, u32[]{:S(2)}, u32[]{:S(2)}) collective-permute-start(s32[1,8]{1,0:T(1,128)} %place.3), channel_id=1, source_target_pairs={{0,16},{8,24},{16,0},{24,8},{1,17},{9,25},{17,1},{25,9},{2,18},{10... | collective-permute-start | bytes 104 | tf_op jit(solution)/shard_map/ppermute | solution.py:440
  4.7 0.7 copy-start
  22.4 25.8 %collective-permute-start.2 = (f32[1032,128]{1,0:T(8,128)S(1)}, f32[1032,128]{1,0:T(8,128)S(1)}, u32[]{:S(2)}, u32[]{:S(2)}) collective-permute-start(f32[1032,128]{1,0:T(8,128)S(1)} %get-tuple-element.31.mine), channel_id=1, source_target_pairs={{0,16},{8,24},{16,0},{24,8},{1,17},{9,25},{17,1},{25,9},{2,18},{10... | collective-permute-start | bytes 1585160 | tf_op jit(solution)/shard_map/ppermute | solution.py:440
  22.5 25.7 %copy-start.1 = (s32[1,8]{1,0:T(1,128)S(1)}, s32[1,8]{1,0:T(1,128)}, u32[]{:S(2)}) copy-start(s32[1,8]{1,0:T(1,128)} %param.5) | copy-start | bytes 100
  26.2 39.1 %collective-permute-start.4 = (f32[1032,128]{1,0:T(8,128)S(1)}, f32[1032,128]{1,0:T(8,128)S(1)}, u32[]{:S(2)}, u32[]{:S(2)}) collective-permute-start(f32[1032,128]{1,0:T(8,128)S(1)} %get-tuple-element.38.rr_low), channel_id=1, source_target_pairs={{0,4},{1,5},{2,6},{3,7},{4,0},{5,1},{6,2},{7,3},{8,12},{9,13},{10,... | collective-permute-start | bytes 1585160 | tf_op jit(solution)/shard_map/ppermute | solution.py:440
  48.2 47.0 %collective-permute-start.3 = (f32[512,512]{1,0:T(8,128)S(1)}, f32[512,512]{1,0:T(8,128)S(1)}, u32[]{:S(2)}, u32[]{:S(2)}) collective-permute-start(f32[512,512]{1,0:T(8,128)S(1)} %get-tuple-element.37.rs), channel_id=1, source_target_pairs={{0,16},{8,24},{16,0},{24,8},{1,17},{9,25},{17,1},{25,9},{2,18},{10... | collective-permute-start | bytes 3145736 | tf_op jit(solution)/shard_map/ppermute | solution.py:440
  48.2 3.7 %collective-permute-start.1 = (s32[3,8]{1,0:T(4,128)S(1)}, s32[3,8]{1,0:T(4,128)S(1)}, u32[]{:S(2)}, u32[]{:S(2)}) collective-permute-start(s32[3,8]{1,0:T(4,128)S(1)} %pad_add_fusion.info.info_a), channel_id=1, source_target_pairs={{0,4},{1,5},{2,6},{3,7},{4,0},{5,1},{6,2},{7,3},{8,12},{9,13},{10,... | collective-permute-start | bytes 296 | tf_op jit(solution)/shard_map/ppermute | solution.py:440
  65.3 33.0 %collective-permute-start.5 = (f32[512,512]{1,0:T(8,128)S(1)}, f32[512,512]{1,0:T(8,128)S(1)}, u32[]{:S(2)}, u32[]{:S(2)}) collective-permute-start(f32[512,512]{1,0:T(8,128)S(1)} %get-tuple-element.41.v_mine), channel_id=1, source_target_pairs={{0,4},{1,5},{2,6},{3,7},{4,0},{5,1},{6,2},{7,3},{8,12},{9,13},{10,... | collective-permute-start | bytes 3145736 | tf_op jit(solution)/shard_map/ppermute | solution.py:440
  96.7 26.1 %collective-permute-start.7 = (f32[512,512]{1,0:T(8,128)S(1)}, f32[512,512]{1,0:T(8,128)S(1)}, u32[]{:S(2)}, u32[]{:S(2)}) collective-permute-start(f32[512,512]{1,0:T(8,128)S(1)} %shard_map.61.v_other), channel_id=1, source_target_pairs={{0,4},{1,5},{2,6},{3,7},{4,0},{5,1},{6,2},{7,3},{8,12},{9,13},{10,... | collective-permute-start | bytes 3145736 | tf_op jit(solution)/shard_map/ppermute | solution.py:440
  98.3 16.2 %collective-permute-start.6 = (f32[640,128]{1,0:T(8,128)S(1)}, f32[640,128]{1,0:T(8,128)S(1)}, u32[]{:S(2)}, u32[]{:S(2)}) collective-permute-start(f32[640,128]{1,0:T(8,128)S(1)} %get-tuple-element.42), channel_id=1, source_target_pairs={{0,16},{8,24},{16,0},{24,8},{1,17},{9,25},{17,1},{25,9},{2,18},{10... | collective-permute-start | bytes 983048 | tf_op jit(solution)/shard_map/ppermute | solution.py:440
  114.5 14.4 %collective-permute-start.9 = (f32[640,128]{1,0:T(8,128)S(1)}, f32[640,128]{1,0:T(8,128)S(1)}, u32[]{:S(2)}, u32[]{:S(2)}) collective-permute-start(f32[640,128]{1,0:T(8,128)S(1)} %collective-permute-done.6.low_a1), channel_id=1, source_target_pairs={{0,4},{1,5},{2,6},{3,7},{4,0},{5,1},{6,2},{7,3},{8,12},{9,13},{10,... | collective-permute-start | bytes 983048 | tf_op jit(solution)/shard_map/ppermute | solution.py:440
  115.0 11.7 %collective-permute-start.8 = (f32[392,128]{1,0:T(8,128)S(1)}, f32[392,128]{1,0:T(8,128)S(1)}, u32[]{:S(2)}, u32[]{:S(2)}) collective-permute-start(f32[392,128]{1,0:T(8,128)S(1)} %get-tuple-element.48), channel_id=1, source_target_pairs={{0,16},{8,24},{16,0},{24,8},{1,17},{9,25},{17,1},{25,9},{2,18},{10... | collective-permute-start | bytes 602120 | tf_op jit(solution)/shard_map/ppermute | solution.py:440
  128.8 6.1 %collective-permute-start.10 = (f32[392,128]{1,0:T(8,128)S(1)}, f32[392,128]{1,0:T(8,128)S(1)}, u32[]{:S(2)}, u32[]{:S(2)}) collective-permute-start(f32[392,128]{1,0:T(8,128)S(1)} %collective-permute-done.8.low_a2), channel_id=1, source_target_pairs={{0,4},{1,5},{2,6},{3,7},{4,0},{5,1},{6,2},{7,3},{8,12},{9,13},{10,... | collective-permute-start | bytes 602120 | tf_op jit(solution)/shard_map/ppermute | solution.py:440

commit v3 on v2

--- a/solution.py
+++ b/solution.py
@@ -17,7 +17,8 @@
 NJ = NS + NB
 BELOW = [(a, b) for a in range(KS) for b in range(a)]
 PACKED = len(BELOW) + KS // 2
-FIRST = PACKED - 3
+FIRST = PACKED - 2
+PLACE_ROW = BLK * PACKED + KS // 2
 VMEM = pl.BlockSpec(memory_space=pltpu.VMEM)
 SMEM = pl.BlockSpec(memory_space=pltpu.SMEM)
 HBM = pl.BlockSpec(memory_space=pltpu.HBM)
@@ -156,26 +157,32 @@
     return jnp.concatenate(inverse, 0)
 
 
-def factor(work, x, lower, inv, corner, ready=None):
+def factor(work, x, lower, inv, corner, gram=None, ready=None):
     ri = lax.broadcasted_iota(jnp.int32, (NS, BLK), 0)
     ci = lax.broadcasted_iota(jnp.int32, (NS, BLK), 1)
 
     def finish(k, inverse):
+        here, then = at(BLK * k), at(BLK * jnp.minimum(k + 1, KS - 1))
+        inv[k] = inverse
+        pair = split(mm3(split(work[then, here]), split(inverse)))
+        corner[...] = work[then, then] - mm3(pair, pair)
+
+    def column(k):
         here = at(BLK * k)
-        inv[k] = inverse
-        lower[:, here] = jnp.where(ri >= ci + BLK * k, mm3(split(work[:, here]), split(inverse)), 0.0)
-        if not isinstance(k, int) or k + 1 < KS:
-            then = at(BLK * jnp.minimum(k + 1, KS - 1))
-            pair = split(lower[then, here])
-            corner[...] = work[then, then] - mm3(pair, pair)
+        inverse = split(inv[k])
+        panel = jnp.where(ri >= ci + BLK * k, mm3(split(work[:, here]), inverse), 0.0)
+        lower[:, here] = panel
+        return here, split(panel), mm3(split(x[:, here]), inverse)
 
     def update(k):
-        here = at(BLK * k)
-        pair = split(lower[:, here])
+        here, pair, done = column(k)
         work[...] = work[...] - mm3(pair, pair)
-        done = mm3(split(x[:, here]), split(inv[k]))
-        x[...] = x[...] - mm3(split(done), pair)
+        new = split(done)
+        x[...] = x[...] - mm3(new, pair)
         x[:, here] = done
+        if gram is not None:
+            top = tuple(v[: gram.shape[0]] for v in new)
+            gram[...] = gram[...] - mm3(top, top)
 
     def step(k, carry):
         inverse = factor_block(corner[...])
@@ -188,7 +195,8 @@
         ready()
     finish(0, inverse)
     lax.fori_loop(1, KS, step, 0)
-    x[:, NS - BLK :] = mm3(split(x[:, NS - BLK :]), split(inv[KS - 1]))
+    here, _, done = column(KS - 1)
+    x[:, here] = done
 
 
 def solve(x, lower, inv):
@@ -227,16 +235,19 @@
     }
 
 
-def leaf_a(front, place, corner, w_out, a, lower, inv, next_block, ss, order, sems):
-    sort_blocks(place, order)
+def leaf_a(front, place_in, corner, w_out, lower, inv, a, next_block, ss, place, order, sems):
     copies = []
     for rows in (slice(0, BLK), slice(BLK, NS)):
         c = pltpu.make_async_copy(front.at[rows, 0:NS], a.at[rows, :], sems.at[len(copies)])
         c.start()
         copies.append(c)
-    for t in range(KB):
+    c = pltpu.make_async_copy(place_in, place, sems.at[len(copies)])
+    c.start()
+    c.wait()
+    sort_blocks(place, order)
+    for t in range(KS):
         c = pltpu.make_async_copy(
-            front.at[at(NS + BLK * order[t]), 0:NS], w_out.at[BLK * t : BLK * t + BLK, :], sems.at[len(copies)]
+            front.at[at(NS + BLK * order[t]), 0:NS], w_out.at[BLK * t : BLK * t + BLK, :], sems.at[1 + len(copies)]
         )
         c.start()
         copies.append(c)
@@ -245,7 +256,7 @@
             c = pltpu.make_async_copy(
                 front.at[at(NS + BLK * order[i]), at(NS + BLK * order[j])],
                 ss.at[BLK * i : BLK * i + BLK, BLK * j : BLK * j + BLK],
-                sems.at[len(copies)],
+                sems.at[1 + len(copies)],
             )
             c.start()
             copies.append(c)
@@ -255,8 +266,8 @@
         for c in copies[1:]:
             c.wait()
 
-    factor(a, w_out, lower, inv, next_block, ready)
-    w = split(w_out[0:NS, :])
+    factor(a, w_out, lower, inv, next_block, ss, ready)
+    w = split(w_out[:, NS - BLK :])
     gram = mm3(w, w)
     blocks = {}
     for i in range(KS):
@@ -268,11 +279,25 @@
         corner[BLK * n : BLK * n + BLK, :] = block
 
     corner[BLK * PACKED :, :] = pack(blocks, out)
-
-
-def leaf_b(front, place, w, rs, rr_all, rr_a, rr_b, f_rs, f_rr, order, sems):
+    lane = lax.broadcasted_iota(jnp.int32, (1, BLK), 1)
+    places = jnp.zeros((1, BLK), f32)
+    for b in range(KB):
+        places = jnp.where(lane == b, place[0, b].astype(f32), places)
+    corner[PLACE_ROW : PLACE_ROW + 1, :] = places
+
+
+def leaf_b(front, place_in, w, lower, inv, rs, rr_all, rr_a, rr_b, wr, f_rs, f_rr, place, order, sems):
+    c = pltpu.make_async_copy(place_in, place, sems.at[KS * KB])
+    c.start()
+    c.wait()
     sort_blocks(place, order)
     copies = []
+    for i in range(KS):
+        c = pltpu.make_async_copy(
+            front.at[at(NS + BLK * order[KS + i]), 0:NS], wr.at[BLK * i : BLK * i + BLK, :], sems.at[KS * KB + 1 + i]
+        )
+        c.start()
+        copies.append(c)
     for i in range(KS):
         for j in range(KB):
             dst = f_rs if j < KS else f_rr
@@ -283,10 +308,13 @@
             )
             c.start()
             copies.append(c)
-    ws, wr = split(w[0:NS, :]), split(w[NS:, :])
-    g_rs = mm3(wr, ws)
-    g_rr = mm3(wr, wr)
-    for c in copies:
+    for c in copies[:KS]:
+        c.wait()
+    solve(wr, lower, inv)
+    ws, wr_pair = split(w[...]), split(wr[...])
+    g_rs = mm3(wr_pair, ws)
+    g_rr = mm3(wr_pair, wr_pair)
+    for c in copies[KS:]:
         c.wait()
     rs[...] = f_rs[...] - g_rs
     f_rr[...] = f_rr[...] - g_rr
@@ -358,24 +386,20 @@
     pair_update(row_blocks(v_mine, v_other), rr_low, canonical(info, order), update, vs)
 
 
-def add_blocks(blocks, spots, ss, x, rr):
+def add_blocks(blocks, spots, ss=None, x=None, rr=None):
     for (i, j), block in blocks.items():
         si, sj = spots[i], spots[j]
 
-        @pl.when((si < KS) & (sj < KS))
-        def _():
-            r, c = at(BLK * si), at(BLK * sj)
-            ss[r, c] = ss[r, c] + block
-
-        @pl.when((si >= KS) & (sj < KS))
-        def _():
-            r, c = at(BLK * (si - KS)), at(BLK * sj)
-            x[r, c] = x[r, c] + block
-
-        @pl.when((si >= KS) & (sj >= KS))
-        def _():
-            r, c = at(BLK * (si - KS)), at(BLK * (sj - KS))
-            rr[r, c] = rr[r, c] + block
+        def add(part, cond, r, c):
+            if part is not None:
+
+                @pl.when(cond)
+                def _():
+                    part[at(BLK * r), at(BLK * c)] = part[at(BLK * r), at(BLK * c)] + block
+
+        add(ss, (si < KS) & (sj < KS), si, sj)
+        add(x, (si >= KS) & (sj < KS), si - KS, sj)
+        add(rr, (si >= KS) & (sj >= KS), si - KS, sj - KS)
 
 
 def join(up_a, up_b, low_a1, low_a2, low_b1, info_a, info_b, ss, x, rr, order):
@@ -404,9 +428,8 @@
     work[...] = ss[...]
     x[...] = x_in[...]
     far = canonical(info, order)[KS:]
-    blocks = unpack_second(low)
-    fill.wait()
-    add_blocks(blocks, far, work, x, buf)
+    add_blocks(unpack_second(low), far, ss=work, x=x)
+
     factor(work, x, lower, inv, next_block)
     outs = [
         pltpu.make_async_copy(lower, panel.at[0:NS, :], sems.at[1]),
@@ -414,12 +437,17 @@
     ]
     for c in outs:
         c.start()
+    fill.wait()
+    add_blocks(unpack_second(low), far, rr=buf)
     pair = split(x[...])
     wide = 2 * BLK
     for t in range(NB // wide):
-        cols = slice(wide * t, wide * t + wide)
-        buf[:, cols] = buf[:, cols] - mm3(pair, tuple(p[cols] for p in pair))
-        c = pltpu.make_async_copy(buf.at[:, cols], update.at[:, cols], sems.at[3 + t])
+        o, e = wide * t, wide * t + wide
+        product = mm3(tuple(p[o:] for p in pair), tuple(p[o:e] for p in pair))
+        buf[o:, o:e] = buf[o:, o:e] - product
+        if e < NB:
+            buf[o:e, e:] = buf[o:e, e:] - product[wide:].T
+        c = pltpu.make_async_copy(buf.at[:, o:e], update.at[:, o:e], sems.at[3 + t])
         c.start()
         outs.append(c)
     for c in outs:
@@ -447,25 +475,27 @@
     tri = sds(BLK * PACKED + 8, BLK)
     tri_a, tri_b = sds(BLK * FIRST, BLK), sds(BLK * (PACKED - FIRST) + 8, BLK)
 
-    pairs_other = partner(place_pairs, "gx")
-    corner, w = call(
-        leaf_a, (tri, sds(NB, NS)), [HBM, SMEM], [VMEM, VMEM],
-        [vmem(NS, NS)] + factor_scratch + [vmem(NS, NS), order, dma((2 + KB + KS * (KS + 1) // 2,))],
+    place = pltpu.SMEM((1, KB), jnp.int32)
+    corner, w, lower, inv = call(
+        leaf_a, (tri, sds(NS, NS), sds(NS, NS), sds(KS, BLK, BLK)), [HBM, HBM], [VMEM] * 4,
+        [vmem(NS, NS), vmem(BLK, BLK), vmem(NS, NS), place, order, dma((3 + KS + KS * (KS + 1) // 2,))],
         (leaf_front, place_pairs), 48)
-    corner_other = partner(after(corner, pairs_other), "gx")
+    corner_other = partner(corner, "gx")
     rs, rr, rr_a, rr_b = call(
-        leaf_b, (sds(NS, NS), tri, tri_a, tri_b), [HBM, SMEM, VMEM], [VMEM] * 4,
-        [vmem(NS, NS), vmem(NS, NS), order, dma((KS * KB,))], (leaf_front, place_pairs, w), 48)
+        leaf_b, (sds(NS, NS), tri, tri_a, tri_b), [HBM, HBM, VMEM, VMEM, VMEM], [VMEM] * 4,
+        [vmem(NS, NS), vmem(NS, NS), vmem(NS, NS), place, order, dma((KS * KB + 1 + KS,))],
+        (leaf_front, place_pairs, w, lower, inv), 48)
     rr_far = partner(rr, "gy")
-    info = jnp.concatenate([place_pairs, pairs_other, place_quads], 0)
-    info_other = partner(info, "gy")
-    corner, info_other = lax.optimization_barrier((corner, info_other))
     rs_other = partner(after(rs, corner_other), "gx")
 
     lower, inv, v_mine = call(
         merge_a, (sds(NS, NS), sds(KS, BLK, BLK), sds(NS, NS)), [VMEM] * 3, [VMEM] * 3,
         [vmem(NS, NS), vmem(BLK, BLK)], (corner, corner_other, rs), us=13)
     v_mine_far = partner(after(v_mine, rr_far), "gy")
+    pairs_other = corner_other[PLACE_ROW : PLACE_ROW + 1, :KB].astype(jnp.int32)
+    info = jnp.concatenate([place_pairs, pairs_other, place_quads], 0)
+    info_other = partner(after(info, lower), "gy")
+    rs_other, info_other = lax.optimization_barrier((rs_other, info_other))
     rr_first = partner(after(rr_a, v_mine_far), "gx")
     v_other = call(merge_b, sds(NS, NS), [VMEM] * 3, VMEM, [], (lower, inv, rs_other))
     v_other_far = partner(v_other, "gy")
@@ -479,7 +509,7 @@
     update_far = call(
         assemble_other, sds(NB, NB), [VMEM] * 3 + [SMEM], VMEM, scratch,
         (v_mine_far, v_other_far, rr_far, info_other))
-    rr_second_far = partner(after(rr_second, update_far, rr_first_far), "gy")
+    rr_second_far = partner(after(rr_second, update_far), "gy")
     ss, x, rr = call(
         join, (sds(NS, NS), sds(NB, NS), sds(NB, NB)), [VMEM] * 5 + [SMEM] * 2, [VMEM] * 3, [order],
         (update, update_far, rr_first, rr_second, rr_first_far, info, info_other))

time: 156 us -> 149 us (0.955)
  waiting for transfers between devices: 72.7 us -> 68.9 us
  starting transfers between devices: 12.9 us -> 10.9 us
    ppermute x11 -> x10, waiting for transfers between devices: 72.7 us -> 68.9 us  [partner(): lax.ppermute(x, axis, [(i, (i + half) % (2 * half)) for i in range(2 * ha...]
    ppermute x11 -> x10, starting transfers between devices: 12.9 us -> 10.9 us  [partner(): lax.ppermute(x, axis, [(i, (i + half) % (2 * half)) for i in range(2 * ha...]
  transfers between devices with their start and end apart: 11 -> 10, of which waited for: 7 -> 6; matrix products, arithmetic and copies ran while one was open for 0% -> 0% of each run, Pallas kernels for 31% -> 22%
where the time goes in v3:
time: 149 us
  waiting for transfers between devices  68.9 us (46%)
  Pallas kernels  67.2 us (45%)
  starting transfers between devices  10.9 us (7%)
    ppermute x10, waiting for transfers between devices, partner(): lax.ppermute(x, axis, [(i, (i + half) % (2 * half)) for i in range(2 * ha...  68.9 us
    pallas_call x8, Pallas kernels, call(): pl.pallas_call(body, out_shape=out, in_specs=ins, out_specs=outs, scratch...  67.2 us
    ppermute x10, starting transfers between devices, partner(): lax.ppermute(x, axis, [(i, (i + half) % (2 * half)) for i in range(2 * ha...  10.9 us
  transfers between devices with their start and end apart: 10, of which 6 were waited for; matrix products, arithmetic and copies ran while one was open for 0% of the time, Pallas kernels for 22%

profile of v3, /device:TPU:0, one launch (start us, length us, event | category | flops | bytes accessed | tf_op | source)
XLA Modules:
  0.0 148.6 jit_solution(8883964183526643454)
XLA Ops:
  0.6 0.0 copy-start
  0.6 0.6 copy-done
  1.3 15.3 %shard_map.58 = (f32[1032,128]{1,0:T(8,128)S(1)}, f32[512,512]{1,0:T(8,128)S(1)}, f32[512,512]{1,0:T(8,128)S(1)}, f32[4,128,128]{2,1,0:T(8,128)S(1)}) custom-call(f32[1536,1536]{1,0:T(8,128)} %front.3, s32[1,8]{1,0:T(1,128)S(1)} %copy-done), custom_call_target="tpu_custom_call" | custom-call | flops 1000 | bytes 1000 | tf_op jit(solution)/shard_map/pallas_call | solution.py:32
  16.6 4.1 %collective-permute-start = (f32[1032,128]{1,0:T(8,128)S(1)}, f32[1032,128]{1,0:T(8,128)S(1)}, u32[]{:S(2)}, u32[]{:S(2)}) collective-permute-start(f32[1032,128]{1,0:T(8,128)S(1)} %get-tuple-element.31.mine), channel_id=1, source_target_pairs={{0,16},{8,24},{16,0},{24,8},{1,17},{9,25},{17,1},{25,9},{2,18},{10... | collective-permute-start | bytes 1585160 | tf_op jit(solution)/shard_map/ppermute | solution.py:468
  20.7 0.0 copy-start.1
  20.7 5.6 %shard_map.59 = (f32[512,512]{1,0:T(8,128)S(1)}, f32[1032,128]{1,0:T(8,128)S(1)}, f32[768,128]{1,0:T(8,128)S(1)}, f32[264,128]{1,0:T(8,128)S(1)}) custom-call(f32[1536,1536]{1,0:T(8,128)} %front.3, s32[1,8]{1,0:T(1,128)S(1)} %copy-done, f32[512,512]{1,0:T(8,128)S(1)} %get-tuple-element.32.w, f32[512,512]{1,0:T(8,128)S(1)} %get-tuple-element.33.lower, ...), custom_call_target="tpu_custom_call" | custom-call | flops 1000 | bytes 1000 | tf_op jit(solution)/shard_map/pallas_call | solution.py:32
  26.3 1.6 %collective-permute-start.3 = (f32[1032,128]{1,0:T(8,128)S(1)}, f32[1032,128]{1,0:T(8,128)S(1)}, u32[]{:S(2)}, u32[]{:S(2)}) collective-permute-start(f32[1032,128]{1,0:T(8,128)S(1)} %get-tuple-element.42.rr_low), channel_id=1, source_target_pairs={{0,4},{1,5},{2,6},{3,7},{4,0},{5,1},{6,2},{7,3},{8,12},{9,13},{10,... | collective-permute-start | bytes 1585160 | tf_op jit(solution)/shard_map/ppermute | solution.py:468
  27.9 16.2 %collective-permute-done.other = f32[1032,128]{1,0:T(8,128)S(1)} collective-permute-done((f32[1032,128]{1,0:T(8,128)S(1)}, f32[1032,128]{1,0:T(8,128)S(1)}, u32[]{:S(2)}, u32[]{:S(2)}) %collective-permute-start) | collective-permute-done | bytes 528416 | tf_op jit(solution)/shard_map/ppermute | solution.py:468
  44.1 0.0 collective-permute-start.1
  44.1 13.2 %shard_map.60 = (f32[512,512]{1,0:T(8,128)S(1)}, f32[4,128,128]{2,1,0:T(8,128)S(1)}, f32[512,512]{1,0:T(8,128)S(1)}) custom-call(f32[1032,128]{1,0:T(8,128)S(1)} %get-tuple-element.31.mine, f32[1032,128]{1,0:T(8,128)S(1)} %collective-permute-done.other, f32[512,512]{1,0:T(8,128)S(1)} %get-tuple-element.39.rs), custom_call_target="tpu_custom_call" | custom-call | flops 1000 | bytes 45501000 | tf_op jit(solution)/shard_map/pallas_call | solution.py:32
  57.2 0.0 collective-permute-done.3.rr_low
  57.2 1.6 %collective-permute-start.4 = (f32[512,512]{1,0:T(8,128)S(1)}, f32[512,512]{1,0:T(8,128)S(1)}, u32[]{:S(2)}, u32[]{:S(2)}) collective-permute-start(f32[512,512]{1,0:T(8,128)S(1)} %get-tuple-element.45.v_mine), channel_id=1, source_target_pairs={{0,4},{1,5},{2,6},{3,7},{4,0},{5,1},{6,2},{7,3},{8,12},{9,13},{10,... | collective-permute-start | bytes 3145736 | tf_op jit(solution)/shard_map/ppermute | solution.py:468
  58.9 0.0 copy-done.1
  58.9 0.5 collective-permute-start.2
  59.4 22.3 %collective-permute-done.2.info.info_b = s32[3,8]{1,0:T(4,128)S(1)} collective-permute-done((s32[3,8]{1,0:T(4,128)S(1)}, s32[3,8]{1,0:T(4,128)S(1)}, u32[]{:S(2)}, u32[]{:S(2)}) %collective-permute-start.2) | collective-permute-done | bytes 128 | tf_op jit(solution)/shard_map/ppermute | solution.py:468
  81.7 10.1 %collective-permute-done.1.rs_other = f32[512,512]{1,0:T(8,128)S(1)} collective-permute-done((f32[512,512]{1,0:T(8,128)S(1)}, f32[512,512]{1,0:T(8,128)S(1)}, u32[]{:S(2)}, u32[]{:S(2)}) %collective-permute-start.1) | collective-permute-done | bytes 1048608 | tf_op jit(solution)/shard_map/ppermute | solution.py:468
  91.8 1.5 shard_map.61.v_other
  93.3 1.4 collective-permute-start.6
  94.6 0.0 collective-permute-done.4.v_mine
  94.6 0.0 collective-permute-start.5
  94.6 5.7 %shard_map.62 = (f32[1536,512]{1,0:T(8,128)}, f32[1024,1024]{1,0:T(8,128)S(1)}) custom-call(f32[512,512]{1,0:T(8,128)S(1)} %get-tuple-element.36.lower, f32[512,512]{1,0:T(8,128)S(1)} %get-tuple-element.45.v_mine, f32[512,512]{1,0:T(8,128)S(1)} %shard_map.61.v_other, f32[1032,128]{1,0:T(8,128)S(1)} %get-tuple-element.42.rr_low, ...), custom_call_target="tpu_custom_call" | custom-call | flops 1000 | bytes 1000 | tf_op jit(solution)/shard_map/pallas_call | solution.py:32
  100.3 12.4 %collective-permute-done.5.low_a1 = f32[768,128]{1,0:T(8,128)S(1)} collective-permute-done((f32[768,128]{1,0:T(8,128)S(1)}, f32[768,128]{1,0:T(8,128)S(1)}, u32[]{:S(2)}, u32[]{:S(2)}) %collective-permute-start.5) | collective-permute-done | bytes 393248 | tf_op jit(solution)/shard_map/ppermute | solution.py:468
  112.8 1.0 collective-permute-start.8
  113.8 0.0 collective-permute-start.7
  113.8 4.8 %collective-permute-done.6.v_other = f32[512,512]{1,0:T(8,128)S(1)} collective-permute-done((f32[512,512]{1,0:T(8,128)S(1)}, f32[512,512]{1,0:T(8,128)S(1)}, u32[]{:S(2)}, u32[]{:S(2)}) %collective-permute-start.6) | collective-permute-done | bytes 1048608 | tf_op jit(solution)/shard_map/ppermute | solution.py:468
  118.6 3.9 %shard_map.63.up_b = f32[1024,1024]{1,0:T(8,128)S(1)} custom-call(f32[512,512]{1,0:T(8,128)S(1)} %collective-permute-done.4.v_mine, f32[512,512]{1,0:T(8,128)S(1)} %collective-permute-done.6.v_other, f32[1032,128]{1,0:T(8,128)S(1)} %collective-permute-done.3.rr_low, s32[3,8]{1,0:T(4,128)S(1)} %collective-permute-done.2.info.info_b), custom_call_target="tpu_custom_call" | custom-call | flops 1000 | bytes 1000 | tf_op jit(solution)/shard_map/pallas_call | solution.py:32
  122.5 0.0 collective-permute-done.7.low_a2
  122.5 0.7 collective-permute-start.9
  123.2 3.2 %collective-permute-done.8.low_b1 = f32[768,128]{1,0:T(8,128)S(1)} collective-permute-done((f32[768,128]{1,0:T(8,128)S(1)}, f32[768,128]{1,0:T(8,128)S(1)}, u32[]{:S(2)}, u32[]{:S(2)}) %collective-permute-start.8) | collective-permute-done | bytes 393248 | tf_op jit(solution)/shard_map/ppermute | solution.py:468
  126.3 2.6 %shard_map.64 = (f32[512,512]{1,0:T(8,128)S(1)}, f32[1024,512]{1,0:T(8,128)S(1)}, f32[1024,1024]{1,0:T(8,128)S(1)}) custom-call(f32[1024,1024]{1,0:T(8,128)S(1)} %get-tuple-element.48.up_a, f32[1024,1024]{1,0:T(8,128)S(1)} %shard_map.63.up_b, f32[768,128]{1,0:T(8,128)S(1)} %collective-permute-done.5.low_a1, f32[264,128]{1,0:T(8,128)S(1)} %collective-permute-done.7.low_a2, ...), custom_call_target="tpu_custom_call" | custom-call | flops 1000 | bytes 1000 | tf_op jit(solution)/shard_map/pallas_call | solution.py:32
  129.0 0.0 collective-permute-done.9.low
  129.0 19.4 %shard_map.65 = (f32[1536,512]{1,0:T(8,128)}, f32[1024,1024]{1,0:T(8,128)}) custom-call(f32[512,512]{1,0:T(8,128)S(1)} %get-tuple-element.53.ss, f32[1024,512]{1,0:T(8,128)S(1)} %get-tuple-element.54.x_in, f32[1024,1024]{1,0:T(8,128)S(1)} %get-tuple-element.55.rr, f32[264,128]{1,0:T(8,128)S(1)} %collective-permute-done.9.low, ...), custom_call_target="tpu_custom_call" | custom-call | flops 1000 | bytes 1000 | tf_op jit(solution)/shard_map/pallas_call | solution.py:32
  (2 shorter events, 0.0 us)
Async XLA Ops:
  0.6 0.7 copy-start
  16.6 27.4 %collective-permute-start = (f32[1032,128]{1,0:T(8,128)S(1)}, f32[1032,128]{1,0:T(8,128)S(1)}, u32[]{:S(2)}, u32[]{:S(2)}) collective-permute-start(f32[1032,128]{1,0:T(8,128)S(1)} %get-tuple-element.31.mine), channel_id=1, source_target_pairs={{0,16},{8,24},{16,0},{24,8},{1,17},{9,25},{17,1},{25,9},{2,18},{10... | collective-permute-start | bytes 1585160 | tf_op jit(solution)/shard_map/ppermute | solution.py:468
  20.7 38.2 %copy-start.1 = (s32[1,8]{1,0:T(1,128)S(1)}, s32[1,8]{1,0:T(1,128)}, u32[]{:S(2)}) copy-start(s32[1,8]{1,0:T(1,128)} %param.5) | copy-start | bytes 100
  26.3 30.9 %collective-permute-start.3 = (f32[1032,128]{1,0:T(8,128)S(1)}, f32[1032,128]{1,0:T(8,128)S(1)}, u32[]{:S(2)}, u32[]{:S(2)}) collective-permute-start(f32[1032,128]{1,0:T(8,128)S(1)} %get-tuple-element.42.rr_low), channel_id=1, source_target_pairs={{0,4},{1,5},{2,6},{3,7},{4,0},{5,1},{6,2},{7,3},{8,12},{9,13},{10,... | collective-permute-start | bytes 1585160 | tf_op jit(solution)/shard_map/ppermute | solution.py:468
  44.1 47.7 %collective-permute-start.1 = (f32[512,512]{1,0:T(8,128)S(1)}, f32[512,512]{1,0:T(8,128)S(1)}, u32[]{:S(2)}, u32[]{:S(2)}) collective-permute-start(f32[512,512]{1,0:T(8,128)S(1)} %get-tuple-element.39.rs), channel_id=1, source_target_pairs={{0,16},{8,24},{16,0},{24,8},{1,17},{9,25},{17,1},{25,9},{2,18},{10... | collective-permute-start | bytes 3145736 | tf_op jit(solution)/shard_map/ppermute | solution.py:468
  57.2 37.4 %collective-permute-start.4 = (f32[512,512]{1,0:T(8,128)S(1)}, f32[512,512]{1,0:T(8,128)S(1)}, u32[]{:S(2)}, u32[]{:S(2)}) collective-permute-start(f32[512,512]{1,0:T(8,128)S(1)} %get-tuple-element.45.v_mine), channel_id=1, source_target_pairs={{0,4},{1,5},{2,6},{3,7},{4,0},{5,1},{6,2},{7,3},{8,12},{9,13},{10,... | collective-permute-start | bytes 3145736 | tf_op jit(solution)/shard_map/ppermute | solution.py:468
  58.9 22.8 %collective-permute-start.2 = (s32[3,8]{1,0:T(4,128)S(1)}, s32[3,8]{1,0:T(4,128)S(1)}, u32[]{:S(2)}, u32[]{:S(2)}) collective-permute-start(s32[3,8]{1,0:T(4,128)S(1)} %pad_add_fusion.info.info_a), channel_id=1, source_target_pairs={{0,4},{1,5},{2,6},{3,7},{4,0},{5,1},{6,2},{7,3},{8,12},{9,13},{10,... | collective-permute-start | bytes 296 | tf_op jit(solution)/shard_map/ppermute | solution.py:468
  93.3 25.4 %collective-permute-start.6 = (f32[512,512]{1,0:T(8,128)S(1)}, f32[512,512]{1,0:T(8,128)S(1)}, u32[]{:S(2)}, u32[]{:S(2)}) collective-permute-start(f32[512,512]{1,0:T(8,128)S(1)} %shard_map.61.v_other), channel_id=1, source_target_pairs={{0,4},{1,5},{2,6},{3,7},{4,0},{5,1},{6,2},{7,3},{8,12},{9,13},{10,... | collective-permute-start | bytes 3145736 | tf_op jit(solution)/shard_map/ppermute | solution.py:468
  94.6 18.1 %collective-permute-start.5 = (f32[768,128]{1,0:T(8,128)S(1)}, f32[768,128]{1,0:T(8,128)S(1)}, u32[]{:S(2)}, u32[]{:S(2)}) collective-permute-start(f32[768,128]{1,0:T(8,128)S(1)} %get-tuple-element.46), channel_id=1, source_target_pairs={{0,16},{8,24},{16,0},{24,8},{1,17},{9,25},{17,1},{25,9},{2,18},{10... | collective-permute-start | bytes 1179656 | tf_op jit(solution)/shard_map/ppermute | solution.py:468
  112.8 13.6 %collective-permute-start.8 = (f32[768,128]{1,0:T(8,128)S(1)}, f32[768,128]{1,0:T(8,128)S(1)}, u32[]{:S(2)}, u32[]{:S(2)}) collective-permute-start(f32[768,128]{1,0:T(8,128)S(1)} %collective-permute-done.5.low_a1), channel_id=1, source_target_pairs={{0,4},{1,5},{2,6},{3,7},{4,0},{5,1},{6,2},{7,3},{8,12},{9,13},{10,... | collective-permute-start | bytes 1179656 | tf_op jit(solution)/shard_map/ppermute | solution.py:468
  113.8 8.7 %collective-permute-start.7 = (f32[264,128]{1,0:T(8,128)S(1)}, f32[264,128]{1,0:T(8,128)S(1)}, u32[]{:S(2)}, u32[]{:S(2)}) collective-permute-start(f32[264,128]{1,0:T(8,128)S(1)} %get-tuple-element.52), channel_id=1, source_target_pairs={{0,16},{8,24},{16,0},{24,8},{1,17},{9,25},{17,1},{25,9},{2,18},{10... | collective-permute-start | bytes 405512 | tf_op jit(solution)/shard_map/ppermute | solution.py:468
  122.5 6.5 %collective-permute-start.9 = (f32[264,128]{1,0:T(8,128)S(1)}, f32[264,128]{1,0:T(8,128)S(1)}, u32[]{:S(2)}, u32[]{:S(2)}) collective-permute-start(f32[264,128]{1,0:T(8,128)S(1)} %collective-permute-done.7.low_a2), channel_id=1, source_target_pairs={{0,4},{1,5},{2,6},{3,7},{4,0},{5,1},{6,2},{7,3},{8,12},{9,13},{10,... | collective-permute-start | bytes 405512 | tf_op jit(solution)/shard_map/ppermute | solution.py:468

commit v4 on v3

--- a/solution.py
+++ b/solution.py
@@ -286,7 +286,7 @@
     corner[PLACE_ROW : PLACE_ROW + 1, :] = places
 
 
-def leaf_b(front, place_in, w, lower, inv, rs, rr_all, rr_a, rr_b, wr, f_rs, f_rr, place, order, sems):
+def leaf_b(front, place_in, w, lower, inv, rs, rs_a, rs_b, rr_all, rr_a, rr_b, wr, f_rs, f_rr, place, order, sems):
     c = pltpu.make_async_copy(place_in, place, sems.at[KS * KB])
     c.start()
     c.wait()
@@ -317,6 +317,8 @@
     for c in copies[KS:]:
         c.wait()
     rs[...] = f_rs[...] - g_rs
+    rs_a[...] = rs[: NS // 2, :]
+    rs_b[...] = rs[NS // 2 :, :]
     f_rr[...] = f_rr[...] - g_rr
 
     def out(n, block):
@@ -371,8 +373,8 @@
     solve(v, lower, inv)
 
 
-def assemble_mine(lower, v_mine, v_other, rr_low, info, panel, update, vs, order):
-    rows = row_blocks(v_mine, v_other)
+def assemble_mine(lower, v_mine, v_first, v_second, rr_low, info, panel, update, vs, order):
+    rows = row_blocks(v_mine, v_first, v_second)
     pair_update(rows, rr_low, canonical(info, order), update, vs)
     panel[0:NS, :] = lower[...]
     for r in range(2):
@@ -382,8 +384,8 @@
             panel[at(BLK * row_of[0, order[KS + i]]), :] = rows[KS * r + i][...]
 
 
-def assemble_other(v_mine, v_other, rr_low, info, update, vs, order):
-    pair_update(row_blocks(v_mine, v_other), rr_low, canonical(info, order), update, vs)
+def assemble_other(v_mine, v_first, v_second, rr_low, info, update, vs, order):
+    pair_update(row_blocks(v_mine, v_first, v_second), rr_low, canonical(info, order), update, vs)
 
 
 def add_blocks(blocks, spots, ss=None, x=None, rr=None):
@@ -423,14 +425,19 @@
 
 
 def last(ss, x_in, rr, low, info, panel, update, work, x, lower, inv, next_block, buf, order, sems):
+    fill_x = pltpu.make_async_copy(x_in, x, sems.at[3 + KB])
     fill = pltpu.make_async_copy(rr, buf, sems.at[0])
+    fill_x.start()
     fill.start()
     work[...] = ss[...]
-    x[...] = x_in[...]
     far = canonical(info, order)[KS:]
-    add_blocks(unpack_second(low), far, ss=work, x=x)
-
-    factor(work, x, lower, inv, next_block)
+    add_blocks(unpack_second(low), far, ss=work)
+
+    def ready():
+        fill_x.wait()
+        add_blocks(unpack_second(low), far, x=x)
+
+    factor(work, x, lower, inv, next_block, ready=ready)
     outs = [
         pltpu.make_async_copy(lower, panel.at[0:NS, :], sems.at[1]),
         pltpu.make_async_copy(x, panel.at[NS:, :], sems.at[2]),
@@ -481,12 +488,13 @@
         [vmem(NS, NS), vmem(BLK, BLK), vmem(NS, NS), place, order, dma((3 + KS + KS * (KS + 1) // 2,))],
         (leaf_front, place_pairs), 48)
     corner_other = partner(corner, "gx")
-    rs, rr, rr_a, rr_b = call(
-        leaf_b, (sds(NS, NS), tri, tri_a, tri_b), [HBM, HBM, VMEM, VMEM, VMEM], [VMEM] * 4,
+    half = NS // 2
+    rs, rs_a, rs_b, rr, rr_a, rr_b = call(
+        leaf_b, (sds(NS, NS), sds(half, NS), sds(half, NS), tri, tri_a, tri_b), [HBM, HBM, VMEM, VMEM, VMEM], [VMEM] * 6,
         [vmem(NS, NS), vmem(NS, NS), vmem(NS, NS), place, order, dma((KS * KB + 1 + KS,))],
         (leaf_front, place_pairs, w, lower, inv), 48)
     rr_far = partner(rr, "gy")
-    rs_other = partner(after(rs, corner_other), "gx")
+    rs_first = partner(after(rs_a, corner_other), "gx")
 
     lower, inv, v_mine = call(
         merge_a, (sds(NS, NS), sds(KS, BLK, BLK), sds(NS, NS)), [VMEM] * 3, [VMEM] * 3,
@@ -495,27 +503,29 @@
     pairs_other = corner_other[PLACE_ROW : PLACE_ROW + 1, :KB].astype(jnp.int32)
     info = jnp.concatenate([place_pairs, pairs_other, place_quads], 0)
     info_other = partner(after(info, lower), "gy")
-    rs_other, info_other = lax.optimization_barrier((rs_other, info_other))
-    rr_first = partner(after(rr_a, v_mine_far), "gx")
-    v_other = call(merge_b, sds(NS, NS), [VMEM] * 3, VMEM, [], (lower, inv, rs_other))
-    v_other_far = partner(v_other, "gy")
+    rs_second = partner(after(rs_b, rs_first, lower), "gx")
+    v_first = call(merge_b, sds(half, NS), [VMEM] * 3, VMEM, [], (lower, inv, rs_first))
+    v_first_far = partner(v_first, "gy")
+    rr_first = partner(after(rr_a, rs_second, v_mine_far, v_first_far), "gx")
+    v_second = call(merge_b, sds(half, NS), [VMEM] * 3, VMEM, [], (lower, inv, rs_second))
+    v_second_far = partner(v_second, "gy")
     scratch = [vmem(NB, NS), order]
     pair_panel, update = call(
-        assemble_mine, (sds(NS + NB, NS), sds(NB, NB)), [VMEM] * 4 + [SMEM], [VMEM] * 2, scratch,
-        (lower, v_mine, v_other, rr, info))
-    rr_first, update = lax.optimization_barrier((rr_first, update))
+        assemble_mine, (sds(NS + NB, NS), sds(NB, NB)), [VMEM] * 5 + [SMEM], [VMEM] * 2, scratch,
+        (lower, v_mine, v_first, v_second, rr, info))
+    rr_first, update, info_other = lax.optimization_barrier((rr_first, update, info_other))
     rr_second = partner(after(rr_b, rr_first), "gx")
     rr_first_far = partner(rr_first, "gy")
     update_far = call(
-        assemble_other, sds(NB, NB), [VMEM] * 3 + [SMEM], VMEM, scratch,
-        (v_mine_far, v_other_far, rr_far, info_other))
+        assemble_other, sds(NB, NB), [VMEM] * 4 + [SMEM], VMEM, scratch,
+        (v_mine_far, v_first_far, v_second_far, rr_far, info_other))
     rr_second_far = partner(after(rr_second, update_far), "gy")
     ss, x, rr = call(
         join, (sds(NS, NS), sds(NB, NS), sds(NB, NB)), [VMEM] * 5 + [SMEM] * 2, [VMEM] * 3, [order],
         (update, update_far, rr_first, rr_second, rr_first_far, info, info_other))
     quad_panel, quad_update = call(
         last, (sds(NS + NB, NS), sds(NB, NB)), [VMEM] * 4 + [SMEM], [HBM, HBM],
-        [vmem(NS, NS), vmem(NB, NS)] + factor_scratch + [vmem(NB, NB), order, dma((3 + KB,))],
+        [vmem(NS, NS), vmem(NB, NS)] + factor_scratch + [vmem(NB, NB), order, dma((4 + KB,))],
         (ss, x, rr, rr_second_far, info_other))
     return pair_panel, quad_panel, quad_update
 

time: 149 us -> 147 us (0.987)
  waiting for transfers between devices: 68.9 us -> 62.5 us
  starting transfers between devices: 10.9 us -> 14.7 us
    ppermute x10 -> x12, waiting for transfers between devices: 68.9 us -> 62.5 us  [partner(): lax.ppermute(x, axis, [(i, (i + half) % (2 * half)) for i in range(2 * ha...]
    ppermute x10 -> x12, starting transfers between devices: 10.9 us -> 14.7 us  [partner(): lax.ppermute(x, axis, [(i, (i + half) % (2 * half)) for i in range(2 * ha...]
    pallas_call x8 -> x9, Pallas kernels: 67.2 us -> 68.3 us  [call(): pl.pallas_call(body, out_shape=out, in_specs=ins, out_specs=outs, scratch...]
  transfers between devices with their start and end apart: 10 -> 12, of which waited for: 6 -> 9; matrix products, arithmetic and copies ran while one was open for 0% -> 0% of each run, Pallas kernels for 22% -> 23%
where the time goes in v4:
time: 147 us
  Pallas kernels  68.3 us (46%)
  waiting for transfers between devices  62.5 us (43%)
  starting transfers between devices  14.7 us (10%)
    pallas_call x9, Pallas kernels, call(): pl.pallas_call(body, out_shape=out, in_specs=ins, out_specs=outs, scratch...  68.3 us
    ppermute x12, waiting for transfers between devices, partner(): lax.ppermute(x, axis, [(i, (i + half) % (2 * half)) for i in range(2 * ha...  62.5 us
    ppermute x12, starting transfers between devices, partner(): lax.ppermute(x, axis, [(i, (i + half) % (2 * half)) for i in range(2 * ha...  14.7 us
  transfers between devices with their start and end apart: 12, of which 9 were waited for; matrix products, arithmetic and copies ran while one was open for 0% of the time, Pallas kernels for 23%

profile of v4, /device:TPU:0, one launch (start us, length us, event | category | flops | bytes accessed | tf_op | source)
XLA Modules:
  0.0 147.1 jit_solution(16542973248441257665)
XLA Ops:
  0.6 0.0 copy-start
  0.6 0.6 copy-done
  1.3 15.3 %shard_map.58 = (f32[1032,128]{1,0:T(8,128)S(1)}, f32[512,512]{1,0:T(8,128)S(1)}, f32[512,512]{1,0:T(8,128)S(1)}, f32[4,128,128]{2,1,0:T(8,128)S(1)}) custom-call(f32[1536,1536]{1,0:T(8,128)} %front.3, s32[1,8]{1,0:T(1,128)S(1)} %copy-done), custom_call_target="tpu_custom_call" | custom-call | flops 1000 | bytes 1000 | tf_op jit(solution)/shard_map/pallas_call | solution.py:32
  16.6 4.1 %collective-permute-start = (f32[1032,128]{1,0:T(8,128)S(1)}, f32[1032,128]{1,0:T(8,128)S(1)}, u32[]{:S(2)}, u32[]{:S(2)}) collective-permute-start(f32[1032,128]{1,0:T(8,128)S(1)} %get-tuple-element.33.mine), channel_id=1, source_target_pairs={{0,16},{8,24},{16,0},{24,8},{1,17},{9,25},{17,1},{25,9},{2,18},{10... | collective-permute-start | bytes 1585160 | tf_op jit(solution)/shard_map/ppermute | solution.py:475
  20.7 5.6 %shard_map.59 = (f32[512,512]{1,0:T(8,128)S(1)}, f32[256,512]{1,0:T(8,128)S(1)}, f32[256,512]{1,0:T(8,128)S(1)}, f32[1032,128]{1,0:T(8,128)S(1)}, f32[768,128]{1,0:T(8,128)S(1)}, /*index=5*/f32[264,128]{1,0:T(8,128)S(1)}) custom-call(f32[1536,1536]{1,0:T(8,128)} %front.3, s32[1,8]{1,0:T(1,128)S(1)} %copy-done, f32[512,512]{1,0:T(8,128)S(1)} %get-tuple-element.34.w, ...), custom_call_target="tpu_custom_call" | custom-call | flops 1000 | bytes 1000 | tf_op jit(solution)/shard_map/pallas_call | solution.py:32
  26.4 0.0 copy-start.1
  26.4 1.6 %collective-permute-start.3 = (f32[1032,128]{1,0:T(8,128)S(1)}, f32[1032,128]{1,0:T(8,128)S(1)}, u32[]{:S(2)}, u32[]{:S(2)}) collective-permute-start(f32[1032,128]{1,0:T(8,128)S(1)} %get-tuple-element.45.rr_low), channel_id=1, source_target_pairs={{0,4},{1,5},{2,6},{3,7},{4,0},{5,1},{6,2},{7,3},{8,12},{9,13},{10,... | collective-permute-start | bytes 1585160 | tf_op jit(solution)/shard_map/ppermute | solution.py:475
  28.0 16.1 %collective-permute-done.other = f32[1032,128]{1,0:T(8,128)S(1)} collective-permute-done((f32[1032,128]{1,0:T(8,128)S(1)}, f32[1032,128]{1,0:T(8,128)S(1)}, u32[]{:S(2)}, u32[]{:S(2)}) %collective-permute-start) | collective-permute-done | bytes 528416 | tf_op jit(solution)/shard_map/ppermute | solution.py:475
  44.1 0.0 collective-permute-start.1
  44.1 13.2 %shard_map.60 = (f32[512,512]{1,0:T(8,128)S(1)}, f32[4,128,128]{2,1,0:T(8,128)S(1)}, f32[512,512]{1,0:T(8,128)S(1)}) custom-call(f32[1032,128]{1,0:T(8,128)S(1)} %get-tuple-element.33.mine, f32[1032,128]{1,0:T(8,128)S(1)} %collective-permute-done.other, f32[512,512]{1,0:T(8,128)S(1)} %get-tuple-element.37.rs), custom_call_target="tpu_custom_call" | custom-call | flops 1000 | bytes 45501000 | tf_op jit(solution)/shard_map/pallas_call | solution.py:32
  57.2 0.0 collective-permute-done.3.rr_low
  57.2 1.6 %collective-permute-start.4 = (f32[512,512]{1,0:T(8,128)S(1)}, f32[512,512]{1,0:T(8,128)S(1)}, u32[]{:S(2)}, u32[]{:S(2)}) collective-permute-start(f32[512,512]{1,0:T(8,128)S(1)} %get-tuple-element.48.v_mine), channel_id=1, source_target_pairs={{0,4},{1,5},{2,6},{3,7},{4,0},{5,1},{6,2},{7,3},{8,12},{9,13},{10,... | collective-permute-start | bytes 3145736 | tf_op jit(solution)/shard_map/ppermute | solution.py:475
  58.9 10.4 %collective-permute-done.1.rs_other = f32[256,512]{1,0:T(8,128)S(1)} collective-permute-done((f32[256,512]{1,0:T(8,128)S(1)}, f32[256,512]{1,0:T(8,128)S(1)}, u32[]{:S(2)}, u32[]{:S(2)}) %collective-permute-start.1) | collective-permute-done | bytes 524320 | tf_op jit(solution)/shard_map/ppermute | solution.py:475
  69.3 0.0 collective-permute-start.2
  69.3 1.2 shard_map.61.v_first
  70.5 1.3 collective-permute-start.5
  71.9 11.5 %collective-permute-done.4.v_mine = f32[512,512]{1,0:T(8,128)S(1)} collective-permute-done((f32[512,512]{1,0:T(8,128)S(1)}, f32[512,512]{1,0:T(8,128)S(1)}, u32[]{:S(2)}, u32[]{:S(2)}) %collective-permute-start.4) | collective-permute-done | bytes 1048608 | tf_op jit(solution)/shard_map/ppermute | solution.py:475
  83.4 10.2 %collective-permute-done.2.rs_other = f32[256,512]{1,0:T(8,128)S(1)} collective-permute-done((f32[256,512]{1,0:T(8,128)S(1)}, f32[256,512]{1,0:T(8,128)S(1)}, u32[]{:S(2)}, u32[]{:S(2)}) %collective-permute-start.2) | collective-permute-done | bytes 524320 | tf_op jit(solution)/shard_map/ppermute | solution.py:475
  93.6 0.0 collective-permute-done.5.v_first
  93.6 1.9 %collective-permute-start.6 = (f32[768,128]{1,0:T(8,128)S(1)}, f32[768,128]{1,0:T(8,128)S(1)}, u32[]{:S(2)}, u32[]{:S(2)}) collective-permute-start(f32[768,128]{1,0:T(8,128)S(1)} %get-tuple-element.49), channel_id=1, source_target_pairs={{0,16},{8,24},{16,0},{24,8},{1,17},{9,25},{17,1},{25,9},{2,18},{10... | collective-permute-start | bytes 1179656 | tf_op jit(solution)/shard_map/ppermute | solution.py:475
  95.5 1.2 shard_map.62.v_second
  96.7 1.3 collective-permute-start.8
  98.1 0.0 copy-done.1
  98.1 0.8 collective-permute-start.7
  98.9 5.7 %shard_map.63 = (f32[1536,512]{1,0:T(8,128)}, f32[1024,1024]{1,0:T(8,128)S(1)}) custom-call(f32[512,512]{1,0:T(8,128)S(1)} %get-tuple-element.38.lower, f32[512,512]{1,0:T(8,128)S(1)} %get-tuple-element.48.v_mine, f32[256,512]{1,0:T(8,128)S(1)} %shard_map.61.v_first, f32[256,512]{1,0:T(8,128)S(1)} %shard_map.62.v_second, ...), custom_call_target="tpu_custom_call" | custom-call | flops 1000 | bytes 1000 | tf_op jit(solution)/shard_map/pallas_call | solution.py:32
  104.6 4.0 %collective-permute-done.7.info.info_b = s32[3,8]{1,0:T(4,128)S(1)} collective-permute-done((s32[3,8]{1,0:T(4,128)S(1)}, s32[3,8]{1,0:T(4,128)S(1)}, u32[]{:S(2)}, u32[]{:S(2)}) %collective-permute-start.7) | collective-permute-done | bytes 128 | tf_op jit(solution)/shard_map/ppermute | solution.py:475
  108.6 5.2 %collective-permute-done.6.low_a1 = f32[768,128]{1,0:T(8,128)S(1)} collective-permute-done((f32[768,128]{1,0:T(8,128)S(1)}, f32[768,128]{1,0:T(8,128)S(1)}, u32[]{:S(2)}, u32[]{:S(2)}) %collective-permute-start.6) | collective-permute-done | bytes 393248 | tf_op jit(solution)/shard_map/ppermute | solution.py:475
  113.8 0.6 collective-permute-start.10
  114.4 0.0 collective-permute-start.9
  114.4 0.0 collective-permute-done.8.v_second
  114.5 3.8 %shard_map.64.up_b = f32[1024,1024]{1,0:T(8,128)S(1)} custom-call(f32[512,512]{1,0:T(8,128)S(1)} %collective-permute-done.4.v_mine, f32[256,512]{1,0:T(8,128)S(1)} %collective-permute-done.5.v_first, f32[256,512]{1,0:T(8,128)S(1)} %collective-permute-done.8.v_second, f32[1032,128]{1,0:T(8,128)S(1)} %collective-permute-done.3.rr_low, ...), custom_call_target="tpu_custom_call" | custom-call | flops 1000 | bytes 1000 | tf_op jit(solution)/shard_map/pallas_call | solution.py:32
  118.3 3.7 %collective-permute-done.9.low_a2 = f32[264,128]{1,0:T(8,128)S(1)} collective-permute-done((f32[264,128]{1,0:T(8,128)S(1)}, f32[264,128]{1,0:T(8,128)S(1)}, u32[]{:S(2)}, u32[]{:S(2)}) %collective-permute-start.9) | collective-permute-done | bytes 135200 | tf_op jit(solution)/shard_map/ppermute | solution.py:475
  122.0 1.4 collective-permute-start.11
  123.4 0.4 collective-permute-done.10.low_b1
  123.8 2.7 %shard_map.65 = (f32[512,512]{1,0:T(8,128)S(1)}, f32[1024,512]{1,0:T(8,128)S(1)}, f32[1024,1024]{1,0:T(8,128)S(1)}) custom-call(f32[1024,1024]{1,0:T(8,128)S(1)} %get-tuple-element.52.up_a, f32[1024,1024]{1,0:T(8,128)S(1)} %shard_map.64.up_b, f32[768,128]{1,0:T(8,128)S(1)} %collective-permute-done.6.low_a1, f32[264,128]{1,0:T(8,128)S(1)} %collective-permute-done.9.low_a2, ...), custom_call_target="tpu_custom_call" | custom-call | flops 1000 | bytes 1000 | tf_op jit(solution)/shard_map/pallas_call | solution.py:32
  126.5 0.9 collective-permute-done.11.low
  127.4 19.6 %shard_map.66 = (f32[1536,512]{1,0:T(8,128)}, f32[1024,1024]{1,0:T(8,128)}) custom-call(f32[512,512]{1,0:T(8,128)S(1)} %get-tuple-element.57.ss, f32[1024,512]{1,0:T(8,128)S(1)} %get-tuple-element.58.x_in, f32[1024,1024]{1,0:T(8,128)S(1)} %get-tuple-element.59.rr, f32[264,128]{1,0:T(8,128)S(1)} %collective-permute-done.11.low, ...), custom_call_target="tpu_custom_call" | custom-call | flops 1000 | bytes 1000 | tf_op jit(solution)/shard_map/pallas_call | solution.py:32
  (2 shorter events, 0.0 us)
Async XLA Ops:
  0.6 0.7 copy-start
  16.6 27.4 %collective-permute-start = (f32[1032,128]{1,0:T(8,128)S(1)}, f32[1032,128]{1,0:T(8,128)S(1)}, u32[]{:S(2)}, u32[]{:S(2)}) collective-permute-start(f32[1032,128]{1,0:T(8,128)S(1)} %get-tuple-element.33.mine), channel_id=1, source_target_pairs={{0,16},{8,24},{16,0},{24,8},{1,17},{9,25},{17,1},{25,9},{2,18},{10... | collective-permute-start | bytes 1585160 | tf_op jit(solution)/shard_map/ppermute | solution.py:475
  26.4 71.7 %copy-start.1 = (s32[1,8]{1,0:T(1,128)S(1)}, s32[1,8]{1,0:T(1,128)}, u32[]{:S(2)}) copy-start(s32[1,8]{1,0:T(1,128)} %param.5) | copy-start | bytes 100
  26.4 30.9 %collective-permute-start.3 = (f32[1032,128]{1,0:T(8,128)S(1)}, f32[1032,128]{1,0:T(8,128)S(1)}, u32[]{:S(2)}, u32[]{:S(2)}) collective-permute-start(f32[1032,128]{1,0:T(8,128)S(1)} %get-tuple-element.45.rr_low), channel_id=1, source_target_pairs={{0,4},{1,5},{2,6},{3,7},{4,0},{5,1},{6,2},{7,3},{8,12},{9,13},{10,... | collective-permute-start | bytes 1585160 | tf_op jit(solution)/shard_map/ppermute | solution.py:475
  44.1 25.2 %collective-permute-start.1 = (f32[256,512]{1,0:T(8,128)S(1)}, f32[256,512]{1,0:T(8,128)S(1)}, u32[]{:S(2)}, u32[]{:S(2)}) collective-permute-start(f32[256,512]{1,0:T(8,128)S(1)} %get-tuple-element.42), channel_id=1, source_target_pairs={{0,16},{8,24},{16,0},{24,8},{1,17},{9,25},{17,1},{25,9},{2,18},{10... | collective-permute-start | bytes 1572872 | tf_op jit(solution)/shard_map/ppermute | solution.py:475
  57.2 26.2 %collective-permute-start.4 = (f32[512,512]{1,0:T(8,128)S(1)}, f32[512,512]{1,0:T(8,128)S(1)}, u32[]{:S(2)}, u32[]{:S(2)}) collective-permute-start(f32[512,512]{1,0:T(8,128)S(1)} %get-tuple-element.48.v_mine), channel_id=1, source_target_pairs={{0,4},{1,5},{2,6},{3,7},{4,0},{5,1},{6,2},{7,3},{8,12},{9,13},{10,... | collective-permute-start | bytes 3145736 | tf_op jit(solution)/shard_map/ppermute | solution.py:475
  69.3 24.3 %collective-permute-start.2 = (f32[256,512]{1,0:T(8,128)S(1)}, f32[256,512]{1,0:T(8,128)S(1)}, u32[]{:S(2)}, u32[]{:S(2)}) collective-permute-start(f32[256,512]{1,0:T(8,128)S(1)} %get-tuple-element.44), channel_id=1, source_target_pairs={{0,16},{8,24},{16,0},{24,8},{1,17},{9,25},{17,1},{25,9},{2,18},{10... | collective-permute-start | bytes 1572872 | tf_op jit(solution)/shard_map/ppermute | solution.py:475
  70.5 23.1 %collective-permute-start.5 = (f32[256,512]{1,0:T(8,128)S(1)}, f32[256,512]{1,0:T(8,128)S(1)}, u32[]{:S(2)}, u32[]{:S(2)}) collective-permute-start(f32[256,512]{1,0:T(8,128)S(1)} %shard_map.61.v_first), channel_id=1, source_target_pairs={{0,4},{1,5},{2,6},{3,7},{4,0},{5,1},{6,2},{7,3},{8,12},{9,13},{10,... | collective-permute-start | bytes 1572872 | tf_op jit(solution)/shard_map/ppermute | solution.py:475
  93.6 20.2 %collective-permute-start.6 = (f32[768,128]{1,0:T(8,128)S(1)}, f32[768,128]{1,0:T(8,128)S(1)}, u32[]{:S(2)}, u32[]{:S(2)}) collective-permute-start(f32[768,128]{1,0:T(8,128)S(1)} %get-tuple-element.49), channel_id=1, source_target_pairs={{0,16},{8,24},{16,0},{24,8},{1,17},{9,25},{17,1},{25,9},{2,18},{10... | collective-permute-start | bytes 1179656 | tf_op jit(solution)/shard_map/ppermute | solution.py:475
  96.7 17.7 %collective-permute-start.8 = (f32[256,512]{1,0:T(8,128)S(1)}, f32[256,512]{1,0:T(8,128)S(1)}, u32[]{:S(2)}, u32[]{:S(2)}) collective-permute-start(f32[256,512]{1,0:T(8,128)S(1)} %shard_map.62.v_second), channel_id=1, source_target_pairs={{0,4},{1,5},{2,6},{3,7},{4,0},{5,1},{6,2},{7,3},{8,12},{9,13},{10,... | collective-permute-start | bytes 1572872 | tf_op jit(solution)/shard_map/ppermute | solution.py:475
  98.1 10.5 %collective-permute-start.7 = (s32[3,8]{1,0:T(4,128)S(1)}, s32[3,8]{1,0:T(4,128)S(1)}, u32[]{:S(2)}, u32[]{:S(2)}) collective-permute-start(s32[3,8]{1,0:T(4,128)S(1)} %pad_add_fusion.info.info_a), channel_id=1, source_target_pairs={{0,4},{1,5},{2,6},{3,7},{4,0},{5,1},{6,2},{7,3},{8,12},{9,13},{10,... | collective-permute-start | bytes 296 | tf_op jit(solution)/shard_map/ppermute | solution.py:475
  113.8 10.0 %collective-permute-start.10 = (f32[768,128]{1,0:T(8,128)S(1)}, f32[768,128]{1,0:T(8,128)S(1)}, u32[]{:S(2)}, u32[]{:S(2)}) collective-permute-start(f32[768,128]{1,0:T(8,128)S(1)} %collective-permute-done.6.low_a1), channel_id=1, source_target_pairs={{0,4},{1,5},{2,6},{3,7},{4,0},{5,1},{6,2},{7,3},{8,12},{9,13},{10,... | collective-permute-start | bytes 1179656 | tf_op jit(solution)/shard_map/ppermute | solution.py:475
  114.4 7.6 %collective-permute-start.9 = (f32[264,128]{1,0:T(8,128)S(1)}, f32[264,128]{1,0:T(8,128)S(1)}, u32[]{:S(2)}, u32[]{:S(2)}) collective-permute-start(f32[264,128]{1,0:T(8,128)S(1)} %get-tuple-element.56), channel_id=1, source_target_pairs={{0,16},{8,24},{16,0},{24,8},{1,17},{9,25},{17,1},{25,9},{2,18},{10... | collective-permute-start | bytes 405512 | tf_op jit(solution)/shard_map/ppermute | solution.py:475
  122.0 5.3 %collective-permute-start.11 = (f32[264,128]{1,0:T(8,128)S(1)}, f32[264,128]{1,0:T(8,128)S(1)}, u32[]{:S(2)}, u32[]{:S(2)}) collective-permute-start(f32[264,128]{1,0:T(8,128)S(1)} %collective-permute-done.9.low_a2), channel_id=1, source_target_pairs={{0,4},{1,5},{2,6},{3,7},{4,0},{5,1},{6,2},{7,3},{8,12},{9,13},{10,... | collective-permute-start | bytes 405512 | tf_op jit(solution)/shard_map/ppermute | solution.py:475
